TPU v7x, 128 devices: a whole 4x4x4 slice. The times are simulated.
128 devices in a mesh: dp: 16 (over y_hi, x, core), space: 8 (over z, y_lo).
Axes of the slice: x: 4, y: 4 (y_hi: 2, y_lo: 2; y = y_hi * 2 + y_lo), z: 4, core: 2. Of those that a mesh axis runs over, the one named last changes fastest.
Arguments:
- volume: bfloat16 [16, 32, 32, 128], P('dp', 'space'), may hold values from -6 to 6
- first_kernel: bfloat16 [3, 3, 3, 4, 64], replicated, may hold values from -0.625 to 0.625
- mid_kernel: bfloat16 [3, 3, 3, 64, 128], replicated, may hold values from -0.15625 to 0.15625
- deep_kernel: bfloat16 [3, 3, 3, 128, 256], replicated, may hold values from -0.109375 to 0.109375
- deep_cotangent: bfloat16 [16, 16, 16, 16, 256], P('dp', 'space'), may hold values from -6 to 6
Outputs:
- deep_output: bfloat16 [16, 16, 16, 16, 256], P('dp', 'space')
- deep_kernel_grad: float32 [3, 3, 3, 128, 256], P(None, None, None, 'space')
- mid_kernel_grad: float32 [3, 3, 3, 64, 128], replicated
All inputs are finite; a program needn't handle non-finite values.
Results may differ from a plain program's by a relative error of at most 0.024.
Values may be sent and summed in bfloat16 or wider, within the bound.
A program may use at most 128 MiB of HBM per device.

v0:
```python
import math

import jax
import jax.numpy as jnp
from jax import lax
from jax.sharding import PartitionSpec as P

SLOPE = 0.3


def padded_2(block, sides, width):
    for axis, dim in sides:
        count = lax.axis_size(axis)
        forward = [(i, i + 1) for i in range(count - 1)]
        backward = [(target, source) for source, target in forward]
        low = lax.ppermute(
            lax.slice_in_dim(block, block.shape[dim] - width, None, axis=dim), axis, forward
        )
        high = lax.ppermute(lax.slice_in_dim(block, 0, width, axis=dim), axis, backward)
        block = jnp.concatenate([low, block, high], axis=dim)
    return block


def activate(value):
    return SLOPE * value + (1.0 - SLOPE) * value * jax.nn.sigmoid(value)


def activate_slope(value):
    sig = jax.nn.sigmoid(value)
    return SLOPE + (1.0 - SLOPE) * (sig + value * sig * (1.0 - sig))


def conv_depth(padded, kernel):
    return lax.conv_general_dilated(
        padded[None],
        kernel,
        (1, 1, 1),
        [(0, 0), (1, 1), (1, 1)],
        dimension_numbers=("NDHWC", "DHWIO", "NDHWC"),
        preferred_element_type=jnp.float32,
    )[0]


def pool_cells(values):
    dd, hh, ww, cc = values.shape
    return values.reshape(dd // 2, 2, hh // 2, 2, ww // 2, 2, cc).mean(axis=(1, 3, 5))


def expand(values):
    return jnp.repeat(jnp.repeat(jnp.repeat(values, 2, 0), 2, 1), 2, 2)


def kernel_grad(padded, cotangent):
    dd, hh, ww, _ = cotangent.shape
    tap_list = []
    for depth_off in range(3):
        for row_off in range(3):
            for col_off in range(3):
                window = padded[
                    depth_off : depth_off + dd, row_off : row_off + hh, col_off : col_off + ww
                ]
                tap_list.append(
                    jnp.einsum(
                        "dhwi,dhwo->io", window, cotangent, preferred_element_type=jnp.float32
                    )
                )
    return jnp.stack(tap_list).reshape(3, 3, 3, padded.shape[-1], cotangent.shape[-1])


def pad_sides(values):
    return jnp.pad(values, ((0, 0), (1, 1), (1, 1), (0, 0)))


def pad_depth(values):
    return jnp.pad(values, ((1, 1), (0, 0), (0, 0), (0, 0)))


def pad_cells(values):
    return jnp.pad(values, ((1, 1), (1, 1), (1, 1), (0, 0)))


def on_device(volume, first_kernel, mid_kernel, deep_kernel, deep_cotangent):
    slab_depth = volume.shape[1]
    side_cells = volume.shape[2]
    in_channels = volume.shape[3] // side_cells
    space_count = lax.axis_size("space")
    space_index = lax.axis_index("space")
    input_field = volume[0].reshape(slab_depth, side_cells, side_cells, in_channels)
    padded = padded_2(input_field, (("space", 0),), 1)
    own_hidden = activate(conv_depth(padded, first_kernel)).astype(jnp.bfloat16)
    hidden = padded_2(own_hidden, (("space", 0),), 1)
    pre_mid = conv_depth(hidden, mid_kernel)
    pooled = pool_cells(activate(pre_mid)).astype(jnp.bfloat16)
    cotangent = deep_cotangent[0].astype(jnp.float32)
    columns = lax.all_to_all(pooled, "space", split_axis=3, concat_axis=0, tiled=True)
    chan_width = columns.shape[3]
    chan_start = space_index * chan_width
    kernel_part = lax.dynamic_slice_in_dim(deep_kernel, chan_start, chan_width, 3)
    partial_value = conv_depth(pad_depth(columns), kernel_part)
    pre_deep = lax.psum_scatter(partial_value, "space", scatter_dimension=0, tiled=True)
    grad_pre = (cotangent * activate_slope(pre_deep)).astype(jnp.bfloat16)
    all_cotangent = lax.all_gather(grad_pre, "space", axis=0, tiled=True)
    deep_grad = kernel_grad(pad_cells(columns), all_cotangent)
    flipped_part = jnp.swapaxes(kernel_part[::-1, ::-1, ::-1], 3, 4)
    back_grad = conv_depth(pad_depth(all_cotangent), flipped_part).astype(jnp.bfloat16)
    pooled_grad = lax.all_to_all(back_grad, "space", split_axis=0, concat_axis=3, tiled=True)
    deep_grad = lax.psum(deep_grad.astype(jnp.bfloat16), "dp").astype(jnp.float32)
    grad_mid = (expand(pooled_grad.astype(jnp.float32)) * 0.125 * activate_slope(pre_mid)).astype(
        jnp.bfloat16
    )
    mid_grad = lax.psum(kernel_grad(pad_sides(hidden), grad_mid), ("dp", "space"))
    device_total = lax.axis_size("dp") * space_count
    cell_count = slab_depth * side_cells * side_cells
    deep_scale = math.sqrt(device_total * cell_count // 8)
    mid_scale = math.sqrt(device_total * cell_count)
    deep_output = activate(pre_deep).astype(jnp.bfloat16)[None]
    return (deep_output, deep_grad / deep_scale, mid_grad / mid_scale)


def solution(mesh):
    in_specs = (P("dp", "space", None, None), P(), P(), P(), P("dp", "space", None, None, None))
    out_specs = (P("dp", "space", None, None, None), P(None, None, None, "space", None), P())
    return jax.shard_map(
        on_device, mesh=mesh, in_specs=in_specs, out_specs=out_specs, check_vma=False
    )
```

profile of v0, /device:TPU:1, one launch (start us, length us, event | category | flops | bytes accessed | tf_op | source)
XLA Modules:
  0.0 628.2 jit_solution(16983838333227108347)
XLA Ops:
  8.2 4.0 collective-permute-start
  13.6 3.4 collective-permute-done.1
  18.2 7.4 %add_convert_fusion = (bf16[4,32,8,5,64]{4,2,3,1,0:T(8,128)(2,1)}, f32[4,32,8,5,64]{4,2,3,1,0:T(8,128)S(1)}, f32[4,32,8,5,64]{4,2,3,1,0:T(8,128)S(1)}, f32[4,32,8,5,64]{4,2,3,1,0:T(8,128)S(1)}) fusion(pred[8,5]{0,1:T(8,128)(4,1)S(1)} %copy-done.21, bf16[3,3,3,4,64]{4,3,2,1,0:T(4,128)(2,1)S(1)} %copy-done.20, bf16[6,32,1,7,2,4]{3,5,4,1,0,2:T(4,128)(2,1)S(1)} %slice.257, ...), kind=kOutput, calls=%fused_computation.31 | convolution fusion | flops 72511488 | bytes 4684328 | tf_op jit(solution)/shard_map/conv_general_dilated | solution.py:34
  27.5 4.8 fusion.30
  32.4 4.3 collective-permute-start.2
  38.0 2.0 collective-permute-done.2
  40.0 7.1 %collective-permute-done.3 = bf16[1,32,32,64]{3,2,1,0:T(8,128)(2,1)S(1)} collective-permute-done((bf16[1,32,32,64]{3,2,1,0:T(8,128)(2,1)S(1)}, bf16[1,32,32,64]{3,2,1,0:T(8,128)(2,1)S(1)}, u32[]{:S(2)}, u32[]{:S(2)}) %collective-permute-start.3) | collective-permute-done | bytes 131104 | tf_op jit(solution)/shard_map/ppermute | solution.py:19
  47.0 1.5 pad_maximum_fusion
  50.6 6.6 %broadcast_multiply_fusion.1 = (f32[4,32,8,5,128]{4,2,3,1,0:T(8,128)S(1)}, f32[4,32,8,5,128]{4,2,3,1,0:T(8,128)S(1)}, f32[4,32,8,5,128]{4,2,3,1,0:T(8,128)S(1)}, f32[4,32,8,5,128]{4,2,3,1,0:T(8,128)}) fusion(bf16[3,3,3,64,128]{4,3,2,1,0:T(8,128)(2,1)S(1)} %copy-done.19, bf16[6,32,1,7,2,64]{5,3,4,1,0,2:T(8,128)(2,1)S(1)} %slice.263, ...), kind=kOutput, calls=%fused_computation.97 | convolution fusion | flops 2225799168 | bytes 12255272 | tf_op jit(solution)/shard_map/conv_general_dilated | solution.py:34
  58.6 2.1 fusion.28
  60.7 2.9 reduce_sum.9
  63.6 1.7 copy.210
  65.3 1.7 reshape.223
  67.0 5.2 all-to-all-start
  72.3 5.5 all-to-all-done
  77.8 1.7 reshape.224
  79.5 1.6 copy.212
  82.5 4.0 copy.321
  86.4 2.8 pad.24.clone
  89.3 5.7 copy.215
  94.9 1.7 slice.267
  96.8 4.5 broadcast_select_fusion
  101.3 2.0 copy.216
  103.3 2.4 slice_bitcast_fusion
  106.2 93.6 %reduce-scatter.2.cloned.1.call-done = f32[2,16,16,256]{3,1,2,0:T(8,128)} async-done(((f32[16,16,16,256]{3,1,2,0:T(8,128)}), f32[2,16,16,256]{3,1,2,0:T(8,128)}) %reduce-scatter.2.cloned.1.call-update) | async-done | bytes 524304 | tf_op jit(solution)/shard_map/reduce_scatter | solution.py:100
  202.1 1.7 copy.240
  205.3 1.5 copy-done.3
  206.8 1.5 slice.271
  208.3 46.0 %all-gather.2.cloned.1.call-done = bf16[16,16,16,256]{3,2,1,0:T(8,128)(2,1)} async-done(((bf16[2,16,16,256]{3,2,1,0:T(8,128)(2,1)}), bf16[16,16,16,256]{3,2,1,0:T(8,128)(2,1)}) %all-gather.2.cloned.1.call-update) | async-done | bytes 2097168 | tf_op jit(solution)/shard_map/all_gather | solution.py:102
  254.3 2.5 copy.219
  257.4 1.6 copy.221
  259.6 22.7 %select_convert_fusion = bf16[16,16,8,3,16]{4,2,3,1,0:T(8,128)(2,1)S(1)} fusion(pred[8,3]{0,1:T(4,128)(4,1)S(1)} %copy-done.22, bf16[18,16,1,7,2,256]{5,3,4,1,0,2:T(8,128)(2,1)S(1)} %slice.269, bf16[18,16,1,8,3,256]{5,3,4,1,0,2:T(8,128)(2,1)S(1)} %copy.221, bf16[3,3,3,128,256]{4,3,2,1,0:T(8,128)(2,1)S(1)} %copy-done, s32[]{:T(128)S(6)} %select_n.3), kind=kOutput, calls=%fused_computation.13 | convolution fusion | flops 1320222720 | bytes 6316548 | tf_op jit(solution)/shard_map/conv_general_dilated | solution.py:34
  283.9 3.1 reshape.225
  287.0 3.4 all-to-all-start.1
  290.6 3.0 fusion.179
  293.5 2.9 fusion.177
  309.9 1.4 fusion.155
  312.5 1.4 fusion.151
  314.0 1.6 fusion.149
  322.2 1.4 fusion.137
  324.9 1.4 fusion.133
  332.1 2.6 copy.314
  334.7 2.6 reshape.222
  340.8 1.5 copy-done.4
  365.0 101.8 %all-reduce.7.cloned.1.call-done = bf16[3,3,3,16,256]{4,3,2,1,0:T(8,128)(2,1)} async-done(((bf16[3,3,3,16,256]{4,3,2,1,0:T(8,128)(2,1)}), bf16[3,3,3,16,256]{4,3,2,1,0:T(8,128)(2,1)}) %all-reduce.7.cloned.1.call-update) | async-done | bytes 221200 | tf_op jit(solution)/shard_map/psum | solution.py:107
  466.9 1.7 convert_multiply_fusion.2
  468.6 150.7 %all-reduce.9.cloned.1.call-done = f32[3,3,3,64,128]{4,3,2,1,0:T(8,128)} async-done(((f32[3,3,3,64,128]{4,3,2,1,0:T(8,128)}), f32[3,3,3,64,128]{4,3,2,1,0:T(8,128)}) %all-reduce.9.cloned.1.call-update) | async-done | bytes 884752 | tf_op jit(solution)/shard_map/psum | solution.py:111
  619.3 2.2 broadcast_multiply_fusion.2
  (143 shorter events, 73.0 us)
Async XLA Ops:
  7.2 89.5 %copy-start = (bf16[3,3,3,128,256]{4,3,2,1,0:T(8,128)(2,1)S(1)}, bf16[3,3,3,128,256]{4,3,2,1,0:T(8,128)(2,1)}, u32[]{:S(2)}) copy-start(bf16[3,3,3,128,256]{4,3,2,1,0:T(8,128)(2,1)} %param.8) | copy-start | bytes 5308420
  7.2 11.0 %copy-start.21 = (pred[8,5]{0,1:T(8,128)(4,1)S(1)}, pred[8,5]{0,1:T(8,128)(4,1)}, u32[]{:S(2)}) copy-start(pred[8,5]{0,1:T(8,128)(4,1)} %constant.63) | copy-start | bytes 124
  7.2 11.0 %copy-start.20 = (bf16[3,3,3,4,64]{4,3,2,1,0:T(4,128)(2,1)S(1)}, bf16[3,3,3,4,64]{4,3,2,1,0:T(4,128)(2,1)}, u32[]{:S(2)}) copy-start(bf16[3,3,3,4,64]{4,3,2,1,0:T(4,128)(2,1)} %param.6) | copy-start | bytes 41476
  8.2 5.3 collective-permute-start
  12.3 4.7 collective-permute-start.1
  32.3 16.2 %copy-start.6 = (bf16[4,32,1,32,64]{4,3,1,2,0:T(8,128)(2,1)}, bf16[4,32,1,32,64]{4,3,1,2,0:T(8,128)(2,1)S(1)}, u32[]{:S(2)}) copy-start(bf16[4,32,1,32,64]{4,3,1,2,0:T(8,128)(2,1)S(1)} %fusion.30) | copy-start | bytes 1572868
  32.4 7.6 %collective-permute-start.2 = (bf16[1,32,32,64]{3,2,1,0:T(8,128)(2,1)S(1)}, bf16[1,32,32,64]{3,2,1,0:T(8,128)(2,1)S(1)}, u32[]{:S(2)}, u32[]{:S(2)}) collective-permute-start(bf16[1,32,32,64]{3,2,1,0:T(8,128)(2,1)S(1)} %get-tuple-element.18), channel_id=1, source_target_pairs={{0,1},{1,2},{2,3},{3,4},{4,5},{5,6},{6,7},{8,9},{9,10},{10,11},{11... | collective-permute-start | bytes 393224 | tf_op jit(solution)/shard_map/ppermute | solution.py:16
  36.7 10.3 %collective-permute-start.3 = (bf16[1,32,32,64]{3,2,1,0:T(8,128)(2,1)S(1)}, bf16[1,32,32,64]{3,2,1,0:T(8,128)(2,1)S(1)}, u32[]{:S(2)}, u32[]{:S(2)}) collective-permute-start(bf16[1,32,32,64]{3,2,1,0:T(8,128)(2,1)S(1)} %get-tuple-element.19), channel_id=1, source_target_pairs={{1,0},{2,1},{3,2},{4,3},{5,4},{6,5},{7,6},{9,8},{10,9},{11,10},{12... | collective-permute-start | bytes 393224 | tf_op jit(solution)/shard_map/ppermute | solution.py:19
  40.0 8.6 %copy-start.16 = (bf16[1,32,32,64]{3,2,1,0:T(8,128)(2,1)}, bf16[1,32,32,64]{3,2,1,0:T(8,128)(2,1)S(1)}, u32[]{:S(2)}) copy-start(bf16[1,32,32,64]{3,2,1,0:T(8,128)(2,1)S(1)} %collective-permute-done.2) | copy-start | bytes 393220
  47.0 1.5 copy-start.14
  49.6 1.0 copy-start.19
  67.0 10.8 %all-to-all-start = ((bf16[8,2,4096]{2,1,0:T(2,128)(2,1)}), bf16[8,2,4096]{2,1,0:T(2,128)(2,1)S(1)}, u32[]{:S(2)}, u32[]{:S(2)}) async-start(bf16[8,2,4096]{2,1,0:T(2,128)(2,1)} %reshape.223), calls=%async_computation | async-start | bytes 262144 | tf_op jit(solution)/shard_map/all_to_all | solution.py:95
  72.3 127.6 %reduce-scatter.2.cloned.1.call-start = ((), (), s32[]{:S(2)}) async-start(), calls=%async_computation.3 | async-start | bytes 4718592 | tf_op jit(solution)/shard_map/reduce_scatter | solution.py:100
  89.3 7.4 %copy-start.22 = (pred[8,3]{0,1:T(4,128)(4,1)S(1)}, pred[8,3]{0,1:T(4,128)(4,1)}, u32[]{:S(2)}) copy-start(pred[8,3]{0,1:T(4,128)(4,1)} %constant.62) | copy-start | bytes 76
  94.9 1.8 copy-start.8
  105.7 94.1 %copy-start.13 = (bf16[1,2,16,16,256]{4,3,2,1,0:T(8,128)(2,1)S(1)}, bf16[1,2,16,16,256]{4,3,2,1,0:T(8,128)(2,1)}, u32[]{:S(2)}) copy-start(bf16[1,2,16,16,256]{4,3,2,1,0:T(8,128)(2,1)} %param.9) | copy-start | bytes 786436
  105.8 148.5 %all-gather.2.cloned.1.call-start = ((), (), s32[]{:S(2)}) async-start(), calls=%async_computation.4 | async-start | bytes 2359296 | tf_op jit(solution)/shard_map/all_gather | solution.py:102
  202.0 2.8 copy-start.9
  205.3 1.5 copy-start.3
  287.0 44.2 %all-to-all-start.1 = ((bf16[8,2,4096]{2,1,0:T(2,128)(2,1)}), bf16[8,2,4096]{2,1,0:T(2,128)(2,1)S(1)}, u32[]{:S(2)}, u32[]{:S(2)}) async-start(bf16[8,2,4096]{2,1,0:T(2,128)(2,1)} %reshape.225), calls=%async_computation.2 | async-start | bytes 262144 | tf_op jit(solution)/shard_map/all_to_all | solution.py:106
  290.4 176.5 %all-reduce.7.cloned.1.call-start = ((), (), s32[]{:S(2)}) async-start(), calls=%async_computation.5 | async-start | bytes 442368 | tf_op jit(solution)/shard_map/psum | solution.py:107
  293.5 2.9 copy-start.2
  330.4 0.7 copy-start.18
  331.1 288.2 %all-reduce.9.cloned.1.call-start = ((), (), s32[]{:S(2)}) async-start(), calls=%async_computation.6 | async-start | bytes 1769472 | tf_op jit(solution)/shard_map/psum | solution.py:111
  337.2 1.6 copy-start.5
  340.6 1.8 copy-start.4
  342.3 1.4 copy-start.10
  345.7 1.2 copy-start.7
  345.7 1.3 copy-start.17
  352.4 1.2 copy-start.11
  359.0 1.0 copy-start.15
  362.6 258.9 %copy-start.1 = (bf16[3,3,3,128,256]{4,3,2,1,0:T(8,128)(2,1)S(1)}, bf16[3,3,3,128,256]{4,3,2,1,0:T(8,128)(2,1)}, u32[]{:S(2)}) copy-start(bf16[3,3,3,128,256]{4,3,2,1,0:T(8,128)(2,1)} %param.8) | copy-start | bytes 5308420
  363.3 0.9 copy-start.12
Sparse Core Ops, SparseCore 0:
  105.9 93.9 reduce-scatter.1
  202.2 52.0 all-gather.1
  331.2 135.5 all-reduce.6
  472.8 146.4 all-reduce.8
where the time goes:
time: 638 us; the launch traced here: 628 us
  waiting for transfers between devices  410 us (64%)
  matrix products  99 us (16%)
  local copies, waits for them, and re-layouts  65.3 us (10%)
  starting transfers between devices  20.2 us (3%)
  other arithmetic  18.8 us (3%)
  between operations  14.7 us (2%)
    psum x1, waiting for transfers between devices, on_device(): lax.psum(kernel_grad(pad_sides(hidden), grad_mid), ('dp', 'space'))  151 us
    psum x1, waiting for transfers between devices, on_device(): lax.psum(deep_grad.astype(jnp.bfloat16), 'dp').astype(jnp.float32)  102 us
    reduce_scatter x1, waiting for transfers between devices, on_device(): lax.psum_scatter(partial_value, 'space', scatter_dimension=0, tiled=True)  93.6 us
    dot_general x54, matrix products, kernel_grad(): jnp.einsum('dhwi,dhwo->io', window, cotangent, preferred_element_type=jnp...  57.9 us
    all_gather x1, waiting for transfers between devices, on_device(): all_cotangent = lax.all_gather(grad_pre, 'space', axis=0, tiled=True)  46 us
    conv_general_dilated x4, matrix products, conv_depth(): lax.conv_general_dilated(padded[None], kernel, (1, 1, 1), [(0, 0), (1, 1)...  41.1 us
    unnamed x55, local copies, waits for them, and re-layouts  22.3 us
    conv_general_dilated x11, local copies, waits for them, and re-layouts, conv_depth(): lax.conv_general_dilated(padded[None], kernel, (1, 1, 1), [(0, 0), (1, 1)...  15.4 us
  transfers between devices with their start and end apart: 10, of which 8 were waited for; matrix products, arithmetic and copies ran while one was open for 12% of the time, Pallas kernels for 0%

commit v1 on v0

v1 whole, which is shorter than its diff:
```python
import functools
import math

import jax
import jax.numpy as jnp
from jax import lax
from jax.experimental import pallas as pl
from jax.experimental.pallas import tpu as pltpu
from jax.sharding import PartitionSpec as P

SLOPE = 0.3
BF = jnp.bfloat16
F32 = jnp.float32
MESH = pl.DeviceIdType.MESH

NS = 8
NQ = 8
CS = 128 // NS
DROWS = 27 * CS
DPIECE = 64
MHALF = 896
MPIECE = MHALF // NS


def sigmoid(z):
    return 0.5 * jnp.tanh(0.5 * z) + 0.5


def act(z):
    return z * (SLOPE + (1.0 - SLOPE) * sigmoid(z))


def act_slope(z):
    s = sigmoid(z)
    return SLOPE + (1.0 - SLOPE) * (s + z * s * (1.0 - s))


def dot(a, b, dims=((1,), (0,))):
    return lax.dot_general(a, b, (dims, ((), ())), preferred_element_type=F32)


def kernel(
    vol_ref, e_ref, km_ref, kd_ref, cot_ref,
    out_ref, dk_ref, mk_ref,
    vhalo, vf, volb, tmat, ybuf, yst, wmid, xpad, xt, slope_mid,
    phalo, pf, pcat, pt, pooled_send, predeep, grad, ghalo, gcat, dbuf, drecv1, dsum1,
    drecv2, dsum2, drecv3, dfull, dother, gmid, mbuf, mrecv1, msum1, mrecv2,
    mrecv3, mfull, mout,
    halo_send, halo_recv, pair_send, pair_recv, ds_send, ds_recv, dq_send, dq_recv,
    dg_send, dg_recv, ms_send, ms_recv, mq_send, mq_recv, mg_send, mg_recv,
):
    s = lax.axis_index("space")
    d = lax.axis_index("dp")
    q = d // 2
    core = d % 2
    other = d + 1 - 2 * core

    def space_peer(k):
        return lax.rem(s + k, NS)

    def dp_peer(k):
        return lax.rem(q + k, NQ) * 2 + core

    up = space_peer(1)
    down = space_peer(NS - 1)

    barrier = pltpu.get_barrier_semaphore()
    for k in range(1, NS):
        pl.semaphore_signal(barrier, inc=1, device_id={"space": space_peer(k)}, device_id_type=MESH)
    for k in range(1, NQ):
        pl.semaphore_signal(barrier, inc=1, device_id={"dp": dp_peer(k)}, device_id_type=MESH)
    pl.semaphore_signal(barrier, inc=1, device_id={"dp": other}, device_id_type=MESH)

    def send(src, dst, ssem, rsem, device):
        copy = pltpu.make_async_remote_copy(
            src_ref=src, dst_ref=dst, send_sem=ssem, recv_sem=rsem,
            device_id=device, device_id_type=MESH,
        )
        copy.start()
        return copy

    def zero_t(i, c):
        tmat[pl.ds(i * 16, 16), :] = jnp.zeros((16, 2048), BF)
        return c

    lax.fori_loop(0, 72, zero_t, 0)
    for ab in range(9):
        base = ab * 128
        for m in range(8):
            lo = slice(2 * m * 128, 2 * m * 128 + 128)
            hi = slice(2 * m * 128 + 128, 2 * m * 128 + 256)
            if m > 0:
                tmat[base + 16 * (m - 1) : base + 16 * m, lo] = e_ref[ab, 0]
            tmat[base + 16 * m : base + 16 * m + 16, lo] = e_ref[ab, 1]
            tmat[base + 16 * m : base + 16 * m + 16, hi] = e_ref[ab, 2]
            if m < 7:
                tmat[base + 16 * (m + 1) : base + 16 * (m + 2), hi] = e_ref[ab, 3]

    for ab in range(9):
        k0 = km_ref[(ab * 3) * 64 : (ab * 3 + 1) * 64, :]
        k1 = km_ref[(ab * 3 + 1) * 64 : (ab * 3 + 2) * 64, :]
        k2 = km_ref[(ab * 3 + 2) * 64 : (ab * 3 + 3) * 64, :]
        z = jnp.zeros((64, 128), BF)
        base = ab * 256
        wmid[base : base + 64, 0:128] = k1
        wmid[base : base + 64, 128:256] = k0
        wmid[base + 64 : base + 128, 0:128] = k2
        wmid[base + 64 : base + 128, 128:256] = k1
        wmid[base + 128 : base + 192, 0:128] = z
        wmid[base + 128 : base + 192, 128:256] = k2
        wmid[base + 192 : base + 256, 0:128] = k0
        wmid[base + 192 : base + 256, 128:256] = z
    for i in range(6):
        xpad[i, 0:16, :] = jnp.zeros((16, 256), BF)
        xpad[i, 528:544, :] = jnp.zeros((16, 256), BF)
    for i in range(4):
        pcat[i, 0:16, :] = jnp.zeros((16, 384), BF)
        pcat[i, 272:288, :] = jnp.zeros((16, 384), BF)
        gcat[i, 0:16, :] = jnp.zeros((16, 768), BF)
        gcat[i, 272:288, :] = jnp.zeros((16, 768), BF)

    pl.semaphore_wait(barrier, NS - 1 + NQ - 1 + 1)

    v_down = send(vol_ref.at[0:2], vhalo.at[1], halo_send.at[0], halo_recv.at[0], {"space": down})
    v_up = send(vol_ref.at[2:4], vhalo.at[0], halo_send.at[1], halo_recv.at[1], {"space": up})
    v_down.wait()
    v_up.wait()

    vf[0:8, :] = jnp.zeros((8, 128), F32)
    vf[264:272, :] = jnp.zeros((8, 128), F32)
    low = jnp.where(s == 0, 0.0, vhalo[0].astype(F32))
    high = jnp.where(s == NS - 1, 0.0, vhalo[1].astype(F32))
    vf[8:72, :] = low.reshape(64, 128)
    vf[72:200, :] = vol_ref[...].astype(F32).reshape(128, 128)
    vf[200:264, :] = high.reshape(64, 128)
    vrow = lax.broadcasted_iota(jnp.int32, (256, 128), 0) % 32
    volb[0] = jnp.where(vrow == 0, 0.0, vf[7:263, :]).astype(BF)
    volb[1] = vf[8:264, :].astype(BF)
    volb[2] = jnp.where(vrow == 31, 0.0, vf[9:265, :]).astype(BF)

    def first(m, c):
        lhs = jnp.concatenate(
            [volb[b, 32 * a : 32 * a + 192, :] for a in range(3) for b in range(3)], axis=1
        )
        col = pl.multiple_of(m * 256, 256)
        ybuf[:, pl.ds(col, 256)] = act(dot(lhs, tmat[:, pl.ds(col, 256)]))
        return c

    lax.fori_loop(0, 8, first, 0)
    ybuf[0:32, :] = jnp.where(s == 0, 0.0, ybuf[0:32, :])
    ybuf[160:192, :] = jnp.where(s == NS - 1, 0.0, ybuf[160:192, :])

    lane = lax.broadcasted_iota(jnp.int32, (32, 128), 1)
    zero = jnp.zeros((32, 128), F32)
    for i in range(6):
        ys = [ybuf[32 * i : 32 * i + 32, 128 * j : 128 * j + 128] for j in range(16)]
        for j in range(16):
            after = ys[j + 1] if j < 15 else zero
            before = ys[j - 1] if j > 0 else zero
            yst[0, pl.ds(j, 32, stride=16), :] = ys[j]
            yst[1, pl.ds(j, 32, stride=16), :] = jnp.where(lane < 64, after, before)
        xpad[i, 16:528, 0:128] = yst[0].astype(BF)
        xpad[i, 16:528, 128:256] = yst[1].astype(BF)

    prow = lax.broadcasted_iota(jnp.int32, (256, 128), 0) % 16
    pf[0:8, :] = jnp.zeros((8, 256), F32)
    pf[264:272, :] = jnp.zeros((8, 256), F32)

    def put_pooled(i, value):
        pf[8:264, 0:128] = value
        pcat[i, 16:272, 0:128] = jnp.where(prow == 0, 0.0, pf[7:263, 0:128]).astype(BF)
        pcat[i, 16:272, 128:256] = value.astype(BF)
        pcat[i, 16:272, 256:384] = jnp.where(prow == 15, 0.0, pf[9:265, 0:128]).astype(BF)

    def mid_plane(i):
        lhs = jnp.concatenate(
            [xpad[i + a, 16 * b : 16 * b + 512, :] for a in range(3) for b in range(3)], axis=1
        )
        pre = dot(lhs, wmid[...])
        slope_mid[i] = 0.125 * act_slope(pre)
        value = act(pre).reshape(16, 2, 16, 256)
        value = value[:, 0] + value[:, 1]
        return (value[:, :, :128] + value[:, :, 128:]).reshape(256, 128)

    p_copies = []
    for plane in range(2):
        pooled = ((mid_plane(2 * plane) + mid_plane(2 * plane + 1)) * 0.125).astype(BF)
        pooled_send[plane] = pooled
        p_copies.append(
            send(
                pooled_send.at[plane], phalo.at[1 - plane], halo_send.at[2 + plane],
                halo_recv.at[2 + plane], {"space": down if plane == 0 else up},
            )
        )
        put_pooled(plane + 1, pooled.astype(F32))

    def deep_taps(plane, a):
        lhs = jnp.concatenate(
            [pcat[plane + a, 16 * b : 16 * b + 256, :] for b in range(3)], axis=1
        )
        return dot(lhs, kd_ref[a * 1152 : (a + 1) * 1152, :])

    predeep[0] = deep_taps(0, 1) + deep_taps(0, 2)
    predeep[1] = deep_taps(1, 0) + deep_taps(1, 1)

    for b in range(3):
        for i in range(6):
            xt[b * 256 : (b + 1) * 256, i * 512 : (i + 1) * 512] = xpad[i, 16 * b : 16 * b + 512, :].T

    for copy in p_copies:
        copy.wait()
    put_pooled(0, jnp.where(s == 0, 0.0, phalo[0].astype(F32)))
    put_pooled(3, jnp.where(s == NS - 1, 0.0, phalo[1].astype(F32)))

    g_copies = []
    for plane in range(2):
        pre = predeep[plane] + deep_taps(plane, 0 if plane == 0 else 2)
        out_ref[plane] = act(pre).astype(BF)
        grad[plane] = (cot_ref[plane].astype(F32) * act_slope(pre)).astype(BF)
        g_copies.append(
            send(
                grad.at[plane], ghalo.at[1 - plane], halo_send.at[4 + plane],
                halo_recv.at[4 + plane], {"space": down if plane == 0 else up},
            )
        )

    grow = lax.broadcasted_iota(jnp.int32, (256, 256), 0) % 16

    def put_grad(i, value):
        pf[8:264, :] = value
        gcat[i, 16:272, 0:256] = jnp.where(grow == 15, 0.0, pf[9:265, :]).astype(BF)
        gcat[i, 16:272, 256:512] = value.astype(BF)
        gcat[i, 16:272, 512:768] = jnp.where(grow == 0, 0.0, pf[7:263, :]).astype(BF)

    put_grad(1, grad[0].astype(F32))
    put_grad(2, grad[1].astype(F32))

    for b in range(3):
        for i in range(4):
            pt[b * 384 : (b + 1) * 384, i * 256 : (i + 1) * 256] = pcat[i, 16 * b : 16 * b + 256, :].T
    gown = grad[...].reshape(512, 256)
    for a in range(3):
        term = dot(pt[:, a * 256 : a * 256 + 512], gown).astype(BF).reshape(9, 128, 256)
        dbuf[0, 9 * a : 9 * a + 9] = term[:, :, :128]
        dbuf[1, 9 * a : 9 * a + 9] = term[:, :, 128:]
    d_pair = send(dbuf.at[1 - core], drecv1, pair_send.at[0], pair_recv.at[0], {"dp": other})

    for copy in g_copies:
        copy.wait()
    put_grad(0, jnp.where(s == 0, 0.0, ghalo[0].astype(F32)))
    put_grad(3, jnp.where(s == NS - 1, 0.0, ghalo[1].astype(F32)))

    def back_plane(plane):
        total = None
        for a in range(3):
            for b in range(3):
                for c in range(3):
                    rows = 16 * (2 - b)
                    tap = (a * 3 + b) * 3 + c
                    term = dot(
                        gcat[plane + 2 - a, rows : rows + 256, 256 * c : 256 * c + 256],
                        kd_ref[tap * 128 : (tap + 1) * 128, :],
                        ((1,), (1,)),
                    )
                    total = term if total is None else total + term
        return total.astype(BF).astype(F32)

    back = [back_plane(0)]

    d_pair.wait()
    dsum1[...] = (dbuf[core].astype(F32) + drecv1[...].astype(F32)).astype(BF)
    d_space = []
    for k in range(1, NS):
        row = pl.multiple_of(space_peer(k) * CS, CS)
        d_space.append(
            send(
                dsum1.at[:, pl.ds(row, CS), :], drecv2.at[k], ds_send.at[k], ds_recv.at[k],
                {"space": space_peer(k)},
            )
        )
    back.append(back_plane(1))

    for plane in range(2):
        wide = jnp.concatenate([back[plane], back[plane]], axis=1).reshape(16, 1, 16, 256)
        for i in range(2):
            value = slope_mid[2 * plane + i].reshape(16, 2, 16, 256) * wide
            row = (2 * plane + i) * 512
            gmid[row : row + 512, :] = value.reshape(512, 256).astype(BF)

    mbuf[27 * 64 : 28 * 64, :] = jnp.zeros((64, 128), BF)

    def mid_grad(a):
        part = dot(xt[:, a * 512 : a * 512 + 2048], gmid[...])
        for b in range(3):
            r = part[b * 256 : (b + 1) * 256]
            row = (a * 3 + b) * 192
            mbuf[row : row + 64, :] = (r[0:64, 128:] + r[192:256, :128]).astype(BF)
            mbuf[row + 64 : row + 128, :] = (r[0:64, :128] + r[64:128, 128:]).astype(BF)
            mbuf[row + 128 : row + 192, :] = (r[64:128, :128] + r[128:192, 128:]).astype(BF)

    mid_grad(0)

    for copy in d_space:
        copy.wait()
    own_row = pl.multiple_of(s * CS, CS)
    total = dsum1[:, pl.ds(own_row, CS), :].astype(F32)
    for k in range(1, NS):
        total = total + drecv2[k].astype(F32)
    dsum2[0:DROWS, :] = total.reshape(DROWS, 128).astype(BF)
    dsum2[DROWS : NQ * DPIECE, :] = jnp.zeros((NQ * DPIECE - DROWS, 128), BF)
    d_dp = []
    for k in range(1, NQ):
        row = pl.multiple_of(lax.rem(q + k, NQ) * DPIECE, DPIECE)
        d_dp.append(
            send(
                dsum2.at[pl.ds(row, DPIECE), :], drecv3.at[k], dq_send.at[k], dq_recv.at[k],
                {"dp": dp_peer(k)},
            )
        )

    mid_grad(1)

    for copy in d_dp:
        copy.wait()
    q_row = pl.multiple_of(q * DPIECE, DPIECE)
    total = dsum2[pl.ds(q_row, DPIECE), :].astype(F32)
    for k in range(1, NQ):
        total = total + drecv3[k].astype(F32)
    dfull[pl.ds(q_row, DPIECE), :] = total.astype(BF)
    d_gather = []
    for k in range(1, NQ):
        d_gather.append(
            send(
                dfull.at[pl.ds(q_row, DPIECE), :], dfull.at[pl.ds(q_row, DPIECE), :],
                dg_send.at[k], dg_recv.at[k], {"dp": dp_peer(k)},
            )
        )

    mid_grad(2)

    m_mine = pl.multiple_of(core * MHALF, MHALF)
    m_theirs = pl.multiple_of((1 - core) * MHALF, MHALF)
    m_pair = send(
        mbuf.at[pl.ds(m_theirs, MHALF), :], mrecv1, pair_send.at[1], pair_recv.at[1], {"dp": other}
    )
    for copy in d_gather:
        copy.wait()
    d_last = send(dfull, dother, pair_send.at[2], pair_recv.at[2], {"dp": other})
    m_pair.wait()
    msum1[...] = (mbuf[pl.ds(m_mine, MHALF), :].astype(F32) + mrecv1[...].astype(F32)).astype(BF)
    m_space = []
    for k in range(1, NS):
        row = pl.multiple_of(space_peer(k) * MPIECE, MPIECE)
        m_space.append(
            send(
                msum1.at[pl.ds(row, MPIECE), :], mrecv2.at[k], ms_send.at[k], ms_recv.at[k],
                {"space": space_peer(k)},
            )
        )
    d_last.wait()
    mine = dfull[0:DROWS, :]
    theirs = dother[0:DROWS, :]
    dk_ref[:, 0:128] = jnp.where(core == 0, mine, theirs)
    dk_ref[:, 128:256] = jnp.where(core == 0, theirs, mine)
    for copy in m_space:
        copy.wait()
    row = pl.multiple_of(s * MPIECE, MPIECE)
    total = msum1[pl.ds(row, MPIECE), :].astype(F32)
    for k in range(1, NS):
        total = total + mrecv2[k].astype(F32)
    mrecv3[q] = total.astype(BF)
    m_dp = []
    for k in range(1, NQ):
        m_dp.append(
            send(mrecv3.at[q], mrecv3.at[q], mq_send.at[k], mq_recv.at[k], {"dp": dp_peer(k)})
        )
    for copy in m_dp:
        copy.wait()
    total = mrecv3[0].astype(F32)
    for k in range(1, NQ):
        total = total + mrecv3[k].astype(F32)
    mfull[pl.ds(row, MPIECE), :] = total.astype(BF)
    m_gather = []
    for k in range(1, NS):
        m_gather.append(
            send(
                mfull.at[pl.ds(row, MPIECE), :], mfull.at[pl.ds(row, MPIECE), :],
                mg_send.at[k], mg_recv.at[k], {"space": space_peer(k)},
            )
        )
    for copy in m_gather:
        copy.wait()
    last = send(
        mfull, mout, pair_send.at[3], pair_recv.at[3], {"dp": other}
    )
    mk_ref[pl.ds(m_mine, MHALF), :] = mfull[...]
    last.wait()
    mk_ref[pl.ds(m_theirs, MHALF), :] = mout[...]


def on_device(volume, first_kernel, mid_kernel, deep_kernel, deep_cotangent):
    k = first_kernel.reshape(9, 3, 4, 64)
    pads = ((0, 0), (0, 0), (0, 0))
    even = jnp.pad(k, (pads[0], (0, 1), *pads[:2]))
    odd = jnp.pad(k, (pads[0], (1, 0), *pads[:2]))
    block = jnp.stack([even, odd], axis=3).reshape(9, 16, 128)
    tiles = jnp.stack(
        [
            jnp.pad(block[:, :4], ((0, 0), (12, 0), (0, 0))),
            jnp.pad(block[:, 4:], ((0, 0), (0, 4), (0, 0))),
            jnp.pad(block[:, :12], ((0, 0), (4, 0), (0, 0))),
            jnp.pad(block[:, 12:], ((0, 0), (0, 12), (0, 0))),
        ],
        axis=1,
    )
    vm = pl.BlockSpec(memory_space=pltpu.VMEM)
    dma = pltpu.SemaphoreType.DMA
    deep_out, deep_grad, mid_grad = pl.pallas_call(
        kernel,
        out_shape=(
            jax.ShapeDtypeStruct((2, 256, 256), BF),
            jax.ShapeDtypeStruct((DROWS, 256), BF),
            jax.ShapeDtypeStruct((2 * MHALF, 128), BF),
        ),
        in_specs=[vm] * 5,
        out_specs=(vm, vm, vm),
        scratch_shapes=[
            pltpu.VMEM((2, 2, 32, 128), BF),
            pltpu.VMEM((272, 128), F32),
            pltpu.VMEM((3, 256, 128), BF),
            pltpu.VMEM((1152, 2048), BF),
            pltpu.VMEM((192, 2048), F32),
            pltpu.VMEM((2, 512, 128), F32),
            pltpu.VMEM((2304, 256), BF),
            pltpu.VMEM((6, 544, 256), BF),
            pltpu.VMEM((768, 3072), BF),
            pltpu.VMEM((4, 512, 256), F32),
            pltpu.VMEM((2, 256, 128), BF),
            pltpu.VMEM((272, 256), F32),
            pltpu.VMEM((4, 288, 384), BF),
            pltpu.VMEM((1152, 1024), BF),
            pltpu.VMEM((2, 256, 128), BF),
            pltpu.VMEM((2, 256, 256), F32),
            pltpu.VMEM((2, 256, 256), BF),
            pltpu.VMEM((2, 256, 256), BF),
            pltpu.VMEM((4, 288, 768), BF),
            pltpu.VMEM((2, 27, 128, 128), BF),
            pltpu.VMEM((27, 128, 128), BF),
            pltpu.VMEM((27, 128, 128), BF),
            pltpu.VMEM((NS, 27, CS, 128), BF),
            pltpu.VMEM((NQ * DPIECE, 128), BF),
            pltpu.VMEM((NQ, DPIECE, 128), BF),
            pltpu.VMEM((NQ * DPIECE, 128), BF),
            pltpu.VMEM((NQ * DPIECE, 128), BF),
            pltpu.VMEM((2048, 256), BF),
            pltpu.VMEM((2 * MHALF, 128), BF),
            pltpu.VMEM((MHALF, 128), BF),
            pltpu.VMEM((MHALF, 128), BF),
            pltpu.VMEM((NS, MPIECE, 128), BF),
            pltpu.VMEM((NQ, MPIECE, 128), BF),
            pltpu.VMEM((MHALF, 128), BF),
            pltpu.VMEM((MHALF, 128), BF),
            dma((6,)), dma((6,)), dma((4,)), dma((4,)),
            *[dma((8,)) for _ in range(12)],
        ],
        compiler_params=pltpu.CompilerParams(
            collective_id=0, has_side_effects=True, vmem_limit_bytes=60 * 1024 * 1024
        ),
    )(
        volume[0],
        tiles,
        mid_kernel.reshape(27 * 64, 128),
        deep_kernel.reshape(27 * 128, 256),
        deep_cotangent.reshape(2, 256, 256),
    )
    deep_scale = math.sqrt(NQ * 2 * NS * 2 * 256)
    mid_scale = math.sqrt(NQ * 2 * NS * 4 * 1024)
    return (
        deep_out.reshape(1, 2, 16, 16, 256),
        deep_grad.astype(F32).reshape(3, 3, 3, CS, 256) / deep_scale,
        mid_grad[: 27 * 64].astype(F32).reshape(3, 3, 3, 64, 128) / mid_scale,
    )


def solution(mesh):
    in_specs = (P("dp", "space", None, None), P(), P(), P(), P("dp", "space", None, None, None))
    out_specs = (P("dp", "space", None, None, None), P(None, None, None, "space", None), P())
    return jax.shard_map(
        on_device, mesh=mesh, in_specs=in_specs, out_specs=out_specs, check_vma=False
    )
```

time: 638 us -> 82.9 us (0.13); the launches traced: 628 us -> 82.7 us
  waiting for transfers between devices: 410 us -> 0 us
  matrix products: 99 us -> 0 us
  Pallas kernels: 0 us -> 75.7 us
  local copies, waits for them, and re-layouts: 65.3 us -> 1.79 us
  starting transfers between devices: 20.2 us -> 0 us
  other arithmetic: 18.8 us -> 4.51 us
  between operations: 14.7 us -> 0.7 us
    psum x2 -> x0, waiting for transfers between devices: 253 us -> none  [the longest x1 151 us: on_device(): lax.psum(kernel_grad(pad_sides(hidden), grad_mid), ('dp', 'space'))]
    reduce_scatter x1 -> x0, waiting for transfers between devices: 93.6 us -> none  [on_device(): lax.psum_scatter(partial_value, 'space', scatter_dimension=0, tiled=True)]
    pallas_call x0 -> x1, Pallas kernels: none -> 75.7 us  [on_device(): pl.pallas_call(kernel, out_shape=(jax.ShapeDtypeStruct((2, 256, 256), BF)...]
    dot_general x54 -> x0, matrix products: 57.9 us -> none  [kernel_grad(): jnp.einsum('dhwi,dhwo->io', window, cotangent, preferred_element_type=jnp...]
    all_gather x1 -> x0, waiting for transfers between devices: 46 us -> none  [on_device(): all_cotangent = lax.all_gather(grad_pre, 'space', axis=0, tiled=True)]
    conv_general_dilated x4 -> x0, matrix products: 41.1 us -> none  [conv_depth(): lax.conv_general_dilated(padded[None], kernel, (1, 1, 1), [(0, 0), (1, 1)...]
    unnamed x55 -> x3, local copies, waits for them, and re-layouts: 22.3 us -> 0.71 us
    conv_general_dilated x11 -> x0, local copies, waits for them, and re-layouts: 15.4 us -> none  [conv_depth(): lax.conv_general_dilated(padded[None], kernel, (1, 1, 1), [(0, 0), (1, 1)...]
  transfers between devices with their start and end apart: 10 -> 0, of which waited for: 8 -> 0; matrix products, arithmetic and copies ran while one was open for 12% -> 0% of each run, Pallas kernels for 0% -> 0%
where the time goes in v1:
time: 82.9 us; the launch traced here: 82.7 us
  Pallas kernels  75.7 us (91%)
  other arithmetic  4.51 us (5%)
  local copies, waits for them, and re-layouts  1.79 us (2%)
    pallas_call x1, Pallas kernels, on_device(): pl.pallas_call(kernel, out_shape=(jax.ShapeDtypeStruct((2, 256, 256), BF)...  75.7 us
    div x1, other arithmetic, on_device(): mid_grad[:27 * 64].astype(F32).reshape(3, 3, 3, 64, 128) / mid_scale  2.03 us
    div x1, other arithmetic, on_device(): deep_grad.astype(F32).reshape(3, 3, 3, CS, 256) / deep_scale  1.73 us

profile of v1, /device:TPU:1, one launch (start us, length us, event | category | flops | bytes accessed | tf_op | source)
XLA Modules:
  0.0 82.7 jit_solution(2562692835715403906)
XLA Ops:
  0.6 0.9 %pad_bitcast_fusion.5 = (bf16[9,4,4,1,64]{4,2,1,0,3:T(4,128)(2,1)S(1)}, bf16[9,4,4,1,64]{4,2,1,0,3:T(4,128)(2,1)S(1)}) fusion(bf16[9,3,4,64]{3,2,1,0:T(4,128)(2,1)} %bitcast.33), kind=kLoop, calls=%fused_computation.9 | loop fusion | bytes 50688 | tf_op jit(solution)/shard_map/stack | solution.py:406
  1.5 0.1 pad_maximum_fusion.1
  1.6 0.1 copy.12
  1.6 0.1 reshape.31
  1.8 0.7 pad_maximum_fusion.e_ref
  2.5 75.7 %shard_map.76 = (bf16[2,256,256]{2,1,0:T(8,128)(2,1)}, bf16[432,256]{1,0:T(8,128)(2,1)}, bf16[1792,128]{1,0:T(8,128)(2,1)}) custom-call(bf16[4,32,128]{2,1,0:T(8,128)(2,1)} %bitcast.32, bf16[9,4,16,128]{3,2,1,0:T(8,128)(2,1)} %pad_maximum_fusion.e_ref, bf16[1728,128]{1,0:T(8,128)(2,1)} %bitcast.29, bf16[3456,256]{1,0:T(8,128)(2,1)} %bitcast.26, ...), custom_call_target="tpu_custom_call" | custom-call | tf_op jit(solution)/shard_map/pallas_call | solution.py:418
  78.2 0.0 copy-start
  78.2 2.0 %convert_multiply_fusion = f32[1728,128]{1,0:T(8,128)} fusion(bf16[1792,128]{1,0:T(8,128)(2,1)} %get-tuple-element.8), kind=kLoop, calls=%fused_computation | loop fusion | flops 442368 | bytes 1327104 | tf_op jit(solution)/shard_map/div | solution.py:481
  80.2 1.7 %convert_multiply_fusion.1 = f32[432,256]{1,0:T(8,128)} fusion(bf16[432,256]{1,0:T(8,128)(2,1)} %get-tuple-element.7), kind=kLoop, calls=%fused_computation.1 | loop fusion | flops 221184 | bytes 663552 | tf_op jit(solution)/shard_map/div | solution.py:480
  82.0 0.0 copy-done
  82.0 0.7 copy.17
  (4 shorter events, 0.1 us)
Async XLA Ops:
  78.2 3.8 %copy-start = (bf16[2,256,256]{2,1,0:T(8,128)(2,1)S(1)}, bf16[2,256,256]{2,1,0:T(8,128)(2,1)}, u32[]{:S(2)}) copy-start(bf16[2,256,256]{2,1,0:T(8,128)(2,1)} %get-tuple-element.6) | copy-start | bytes 786436

commit v2 on v1

v2 whole, which is shorter than its diff:
```python
import functools
import math

import jax
import jax.numpy as jnp
from jax import lax
from jax.experimental import pallas as pl
from jax.experimental.pallas import tpu as pltpu
from jax.sharding import PartitionSpec as P

SLOPE = 0.3
BF = jnp.bfloat16
F32 = jnp.float32
MESH = pl.DeviceIdType.MESH

NS = 8
NQ = 8
CS = 128 // NS
DROWS = 27 * CS
DPIECE = 64
MROWS = 28 * 64
MHALF = MROWS // 2
MPARTS = ((0, 512), (512, 512), (1024, 768))
MONE = MHALF // NS


def sigmoid(z):
    return 0.5 * jnp.tanh(0.5 * z) + 0.5


def act(z):
    return z * (SLOPE + (1.0 - SLOPE) * sigmoid(z))


def act_slope(z):
    s = sigmoid(z)
    return SLOPE + (1.0 - SLOPE) * (s + z * s * (1.0 - s))


def dot(a, b, dims=((1,), (0,))):
    return lax.dot_general(a, b, (dims, ((), ())), preferred_element_type=F32)


def kernel(
    fk_ref, vol_hbm, km_hbm, kd_hbm, cot_hbm,
    out_ref, dk_ref, mk_ref,
    vol_ref, km_ref, kd_ref, cot_ref,
    vhalo, ef, vf, volb, tmat, ybuf, yst, wmid, xpad, xt, pre_mid, slope_mid,
    phalo, pf, pcat, pt, pooled_send, predeep, grad, bsend, bhalo, gcat, dbuf, drecv1, dsum1,
    drecv2, dsum2, drecv3, dfull, dother, gmid, mbuf, mrecv1, msum1, mrecv2,
    mrecv3, mfull, mout,
    load_sem, halo_send, halo_recv, pair_send, pair_recv, ds_send, ds_recv, dq_send, dq_recv,
    dg_send, dg_recv, mp_send, mp_recv, ms_send, ms_recv, mq_send, mq_recv, mg_send, mg_recv,
    mo_send, mo_recv,
):
    s = lax.axis_index("space")
    d = lax.axis_index("dp")
    q = d // 2
    core = d % 2
    other = d + 1 - 2 * core

    def space_peer(k):
        return lax.rem(s + k, NS)

    def dp_peer(k):
        return lax.rem(q + k, NQ) * 2 + core

    up = space_peer(1)
    down = space_peer(NS - 1)

    barrier = pltpu.get_barrier_semaphore()
    for k in (1, NS - 1, *range(2, NS - 1)):
        pl.semaphore_signal(barrier, inc=1, device_id={"space": space_peer(k)}, device_id_type=MESH)
    for k in range(1, NQ):
        pl.semaphore_signal(barrier, inc=1, device_id={"dp": dp_peer(k)}, device_id_type=MESH)
    pl.semaphore_signal(barrier, inc=1, device_id={"dp": other}, device_id_type=MESH)

    loads = []
    for i, (src, dst) in enumerate(
        ((vol_hbm, vol_ref), (km_hbm, km_ref), (kd_hbm, kd_ref), (cot_hbm, cot_ref))
    ):
        loads.append(pltpu.make_async_copy(src, dst, load_sem.at[i]))
        loads[-1].start()

    def send(src, dst, ssem, rsem, device):
        copy = pltpu.make_async_remote_copy(
            src_ref=src, dst_ref=dst, send_sem=ssem, recv_sem=rsem,
            device_id=device, device_id_type=MESH,
        )
        copy.start()
        return copy

    def zero_t(i, c):
        tmat[pl.ds(i * 16, 16), :] = jnp.zeros((16, 2048), BF)
        return c

    lax.fori_loop(0, 72, zero_t, 0)
    ef[...] = jnp.zeros((48, 128), F32)
    for ab in range(9):
        base = ab * 128
        for c in range(3):
            tap = fk_ref[ab * 3 + c].astype(F32)
            ef[16 + 4 * c : 20 + 4 * c, 0:64] = tap
            ef[20 + 4 * c : 24 + 4 * c, 64:128] = tap
        tiles = [ef[o : o + 16, :].astype(BF) for o in (4, 20, 12, 28)]
        for m in range(8):
            lo = slice(2 * m * 128, 2 * m * 128 + 128)
            hi = slice(2 * m * 128 + 128, 2 * m * 128 + 256)
            if m > 0:
                tmat[base + 16 * (m - 1) : base + 16 * m, lo] = tiles[0]
            tmat[base + 16 * m : base + 16 * m + 16, lo] = tiles[1]
            tmat[base + 16 * m : base + 16 * m + 16, hi] = tiles[2]
            if m < 7:
                tmat[base + 16 * (m + 1) : base + 16 * (m + 2), hi] = tiles[3]

    loads[0].wait()
    pl.semaphore_wait(barrier, NS - 1 + NQ - 1 + 1)

    v_down = send(vol_ref.at[0:2], vhalo.at[1], halo_send.at[0], halo_recv.at[0], {"space": down})
    v_up = send(vol_ref.at[2:4], vhalo.at[0], halo_send.at[1], halo_recv.at[1], {"space": up})

    loads[1].wait()
    for ab in range(9):
        k0 = km_ref[(ab * 3) * 64 : (ab * 3 + 1) * 64, :]
        k1 = km_ref[(ab * 3 + 1) * 64 : (ab * 3 + 2) * 64, :]
        k2 = km_ref[(ab * 3 + 2) * 64 : (ab * 3 + 3) * 64, :]
        z = jnp.zeros((64, 128), BF)
        base = ab * 256
        wmid[base : base + 64, 0:128] = k1
        wmid[base : base + 64, 128:256] = k0
        wmid[base + 64 : base + 128, 0:128] = k2
        wmid[base + 64 : base + 128, 128:256] = k1
        wmid[base + 128 : base + 192, 0:128] = z
        wmid[base + 128 : base + 192, 128:256] = k2
        wmid[base + 192 : base + 256, 0:128] = k0
        wmid[base + 192 : base + 256, 128:256] = z
    for i in range(6):
        xpad[i, 0:16, :] = jnp.zeros((16, 256), BF)
        xpad[i, 528:544, :] = jnp.zeros((16, 256), BF)
    for i in range(4):
        pcat[i, 0:16, :] = jnp.zeros((16, 384), BF)
        pcat[i, 272:288, :] = jnp.zeros((16, 384), BF)
    for i in range(2):
        gcat[i, 0:16, :] = jnp.zeros((16, 768), BF)
        gcat[i, 272:288, :] = jnp.zeros((16, 768), BF)
    mbuf[27 * 64 : 28 * 64, :] = jnp.zeros((64, 128), BF)

    def put_volume(row, value):
        rows = value.shape[0]
        edge = lax.broadcasted_iota(jnp.int32, (rows, 128), 0) % 32
        vf[8 : 8 + rows, :] = value
        volb[0, row : row + rows, :] = jnp.where(edge == 0, 0.0, vf[7 : 7 + rows, :]).astype(BF)
        volb[1, row : row + rows, :] = value.astype(BF)
        volb[2, row : row + rows, :] = jnp.where(edge == 31, 0.0, vf[9 : 9 + rows, :]).astype(BF)

    vf[0:8, :] = jnp.zeros((8, 128), F32)
    vf[136:144, :] = jnp.zeros((8, 128), F32)
    put_volume(64, vol_ref[...].astype(F32).reshape(128, 128))

    def first(plane):
        def step(m, c):
            lhs = jnp.concatenate(
                [
                    volb[b, 32 * (plane + a) : 32 * (plane + a) + 64, :]
                    for a in range(3)
                    for b in range(3)
                ],
                axis=1,
            )
            col = pl.multiple_of(m * 256, 256)
            ybuf[32 * plane : 32 * plane + 64, pl.ds(col, 256)] = act(
                dot(lhs, tmat[:, pl.ds(col, 256)])
            )
            return c

        lax.fori_loop(0, 8, step, 0)

    lane = lax.broadcasted_iota(jnp.int32, (32, 128), 1)
    zero = jnp.zeros((32, 128), F32)

    def put_hidden(i):
        ys = [ybuf[32 * i : 32 * i + 32, 128 * j : 128 * j + 128] for j in range(16)]
        for j in range(16):
            after = ys[j + 1] if j < 15 else zero
            before = ys[j - 1] if j > 0 else zero
            yst[0, pl.ds(j, 32, stride=16), :] = ys[j]
            yst[1, pl.ds(j, 32, stride=16), :] = jnp.where(lane < 64, after, before)
        xpad[i, 16:528, 0:128] = yst[0].astype(BF)
        xpad[i, 16:528, 128:256] = yst[1].astype(BF)

    first(2)
    put_hidden(2)
    put_hidden(3)

    v_up.wait()
    put_volume(0, jnp.where(s == 0, 0.0, vhalo[0].astype(F32)).reshape(64, 128))
    first(0)
    ybuf[0:32, :] = jnp.where(s == 0, 0.0, ybuf[0:32, :])
    put_hidden(0)
    put_hidden(1)

    prow = lax.broadcasted_iota(jnp.int32, (256, 128), 0) % 16
    pf[0:8, :] = jnp.zeros((8, 256), F32)
    pf[264:272, :] = jnp.zeros((8, 256), F32)

    def put_pooled(i, value):
        pf[8:264, 0:128] = value
        pcat[i, 16:272, 0:128] = jnp.where(prow == 0, 0.0, pf[7:263, 0:128]).astype(BF)
        pcat[i, 16:272, 128:256] = value.astype(BF)
        pcat[i, 16:272, 256:384] = jnp.where(prow == 15, 0.0, pf[9:265, 0:128]).astype(BF)

    def mid_plane(i):
        lhs = jnp.concatenate(
            [xpad[i + a, 16 * b : 16 * b + 512, :] for a in range(3) for b in range(3)], axis=1
        )
        pre = dot(lhs, wmid[...])
        pre_mid[i] = pre
        value = act(pre).reshape(16, 2, 16, 256)
        value = value[:, 0] + value[:, 1]
        return (value[:, :, :128] + value[:, :, 128:]).reshape(256, 128)

    p_copies = []

    def pool(plane):
        pooled = ((mid_plane(2 * plane) + mid_plane(2 * plane + 1)) * 0.125).astype(BF)
        pooled_send[plane] = pooled
        p_copies.append(
            send(
                pooled_send.at[plane], phalo.at[1 - plane], halo_send.at[2 + plane],
                halo_recv.at[2 + plane], {"space": down if plane == 0 else up},
            )
        )
        put_pooled(plane + 1, pooled.astype(F32))

    pool(0)

    v_down.wait()
    put_volume(192, jnp.where(s == NS - 1, 0.0, vhalo[1].astype(F32)).reshape(64, 128))
    first(4)
    ybuf[160:192, :] = jnp.where(s == NS - 1, 0.0, ybuf[160:192, :])
    put_hidden(4)
    put_hidden(5)
    pool(1)

    loads[2].wait()

    def deep_taps(plane, a):
        lhs = jnp.concatenate(
            [pcat[plane + a, 16 * b : 16 * b + 256, :] for b in range(3)], axis=1
        )
        return dot(lhs, kd_ref[a * 1152 : (a + 1) * 1152, :])

    predeep[0] = deep_taps(0, 1) + deep_taps(0, 2)
    predeep[1] = deep_taps(1, 0) + deep_taps(1, 1)

    for b in range(3):
        for i in range(6):
            xt[b * 256 : (b + 1) * 256, i * 512 : (i + 1) * 512] = xpad[i, 16 * b : 16 * b + 512, :].T

    def slopes(i, c):
        slope_mid[i] = 0.125 * act_slope(pre_mid[i])
        return c

    lax.fori_loop(0, 4, slopes, 0)

    def put_turned(i):
        for b in range(3):
            pt[b * 384 : (b + 1) * 384, i * 256 : (i + 1) * 256] = pcat[i, 16 * b : 16 * b + 256, :].T

    put_turned(1)
    put_turned(2)
    loads[3].wait()

    grow = lax.broadcasted_iota(jnp.int32, (256, 256), 0) % 16

    def put_grad(i, value):
        pf[8:264, :] = value
        gcat[i, 16:272, 0:256] = jnp.where(grow == 15, 0.0, pf[9:265, :]).astype(BF)
        gcat[i, 16:272, 256:512] = value.astype(BF)
        gcat[i, 16:272, 512:768] = jnp.where(grow == 0, 0.0, pf[7:263, :]).astype(BF)

    def back_taps(plane, a):
        total = None
        for b in range(3):
            for c in range(3):
                rows = 16 * (2 - b)
                tap = (a * 3 + b) * 3 + c
                term = dot(
                    gcat[plane, rows : rows + 256, 256 * c : 256 * c + 256],
                    kd_ref[tap * 128 : (tap + 1) * 128, :],
                    ((1,), (1,)),
                )
                total = term if total is None else total + term
        return total

    b_copies = []
    for plane in (1, 0):
        p_copies[1 - plane].wait()
        if plane == 1:
            put_pooled(3, jnp.where(s == NS - 1, 0.0, phalo[1].astype(F32)))
        else:
            put_pooled(0, jnp.where(s == 0, 0.0, phalo[0].astype(F32)))
        pre = predeep[plane] + deep_taps(plane, 0 if plane == 0 else 2)
        predeep[plane] = pre
        value = (cot_ref[plane].astype(F32) * act_slope(pre)).astype(BF)
        grad[plane] = value
        put_grad(plane, value.astype(F32))
        bsend[plane] = back_taps(plane, 0 if plane == 0 else 2).astype(BF)
        b_copies.append(
            send(
                bsend.at[plane], bhalo.at[1 - plane], halo_send.at[4 + plane],
                halo_recv.at[4 + plane], {"space": down if plane == 0 else up},
            )
        )

    put_turned(0)
    put_turned(3)
    gown = grad[...].reshape(512, 256)
    for a in range(3):
        term = dot(pt[:, a * 256 : a * 256 + 512], gown).astype(BF).reshape(9, 128, 256)
        dbuf[0, 9 * a : 9 * a + 9] = term[:, :, :128]
        dbuf[1, 9 * a : 9 * a + 9] = term[:, :, 128:]
    d_pair = send(dbuf.at[1 - core], drecv1, pair_send.at[0], pair_recv.at[0], {"dp": other})

    back = [back_taps(0, 1) + back_taps(1, 0), back_taps(1, 1) + back_taps(0, 2)]

    d_pair.wait()
    dsum1[...] = (dbuf[core].astype(F32) + drecv1[...].astype(F32)).astype(BF)
    d_space = []
    for k in range(1, NS):
        row = pl.multiple_of(space_peer(k) * CS, CS)
        d_space.append(
            send(
                dsum1.at[:, pl.ds(row, CS), :], drecv2.at[k], ds_send.at[k], ds_recv.at[k],
                {"space": space_peer(k)},
            )
        )

    out_ref[...] = act(predeep[...]).astype(BF)

    for plane in (1, 0):
        b_copies[plane].wait()
        edge = s == (0 if plane == 0 else NS - 1)
        total = back[plane] + jnp.where(edge, 0.0, bhalo[plane].astype(F32))
        total = total.astype(BF).astype(F32)
        wide = jnp.concatenate([total, total], axis=1).reshape(16, 1, 16, 256)
        for i in range(2):
            value = slope_mid[2 * plane + i].reshape(16, 2, 16, 256) * wide
            row = (2 * plane + i) * 512
            gmid[row : row + 512, :] = value.reshape(512, 256).astype(BF)

    def mid_grad(a):
        part = dot(xt[:, a * 512 : a * 512 + 2048], gmid[...])
        for b in range(3):
            r = part[b * 256 : (b + 1) * 256]
            row = (a * 3 + b) * 192
            mbuf[row : row + 64, :] = (r[0:64, 128:] + r[192:256, :128]).astype(BF)
            mbuf[row + 64 : row + 128, :] = (r[0:64, :128] + r[64:128, 128:]).astype(BF)
            mbuf[row + 128 : row + 192, :] = (r[64:128, :128] + r[128:192, 128:]).astype(BF)

    def m_pair(p):
        base, rows = MPARTS[p]
        half = rows // 2
        theirs = pl.multiple_of(base + (1 - core) * half, 16)
        return send(
            mbuf.at[pl.ds(theirs, half), :], mrecv1.at[base // 2 : base // 2 + half, :],
            mp_send.at[p], mp_recv.at[p], {"dp": other},
        )

    def m_space(p, pair):
        base, rows = MPARTS[p]
        half, one = rows // 2, rows // 2 // NS
        lo = base // 2
        pair.wait()
        mine = pl.multiple_of(base + core * half, 16)
        msum1[lo : lo + half, :] = (
            mbuf[pl.ds(mine, half), :].astype(F32) + mrecv1[lo : lo + half, :].astype(F32)
        ).astype(BF)
        copies = []
        for k in range(1, NS):
            row = pl.multiple_of(lo + space_peer(k) * one, 16)
            copies.append(
                send(
                    msum1.at[pl.ds(row, one), :], mrecv2.at[k, lo // NS : lo // NS + one, :],
                    ms_send.at[p, k], ms_recv.at[p, k], {"space": space_peer(k)},
                )
            )
        return copies

    def m_dp(p, copies):
        base, rows = MPARTS[p]
        one = rows // 2 // NS
        lo = base // 2
        for copy in copies:
            copy.wait()
        row = pl.multiple_of(lo + s * one, 16)
        total = msum1[pl.ds(row, one), :].astype(F32)
        for k in range(1, NS):
            total = total + mrecv2[k, lo // NS : lo // NS + one, :].astype(F32)
        part = mrecv3.at[q, lo // NS : lo // NS + one, :]
        part[...] = total.astype(BF)
        return [
            send(part, part, mq_send.at[p, k], mq_recv.at[p, k], {"dp": dp_peer(k)})
            for k in range(1, NQ)
        ]

    def m_gather(p, copies):
        base, rows = MPARTS[p]
        one = rows // 2 // NS
        lo = base // 2
        for copy in copies:
            copy.wait()
        total = mrecv3[0, lo // NS : lo // NS + one, :].astype(F32)
        for k in range(1, NQ):
            total = total + mrecv3[k, lo // NS : lo // NS + one, :].astype(F32)
        row = pl.multiple_of(lo + s * one, 16)
        mfull[pl.ds(row, one), :] = total.astype(BF)
        part = mfull.at[pl.ds(row, one), :]
        return [
            send(part, part, mg_send.at[p, k], mg_recv.at[p, k], {"space": space_peer(k)})
            for k in range(1, NS)
        ]

    def m_last(p, copies):
        base, rows = MPARTS[p]
        half = rows // 2
        lo = base // 2
        for copy in copies:
            copy.wait()
        copy = send(
            mfull.at[lo : lo + half, :], mout.at[lo : lo + half, :], mo_send.at[p], mo_recv.at[p],
            {"dp": other},
        )
        mk_ref[pl.ds(pl.multiple_of(base + core * half, 16), half), :] = mfull[lo : lo + half, :]
        return copy

    def m_store(p, copy):
        base, rows = MPARTS[p]
        half = rows // 2
        lo = base // 2
        copy.wait()
        theirs = pl.multiple_of(base + (1 - core) * half, 16)
        mk_ref[pl.ds(theirs, half), :] = mout[lo : lo + half, :]

    mid_grad(0)
    m0 = m_pair(0)
    mid_grad(1)
    m1 = m_pair(1)
    m0 = m_space(0, m0)
    mid_grad(2)
    m2 = m_pair(2)
    m1 = m_space(1, m1)
    m2 = m_space(2, m2)

    m0 = m_dp(0, m0)
    m1 = m_dp(1, m1)

    for copy in d_space:
        copy.wait()
    own_row = pl.multiple_of(s * CS, CS)
    total = dsum1[:, pl.ds(own_row, CS), :].astype(F32)
    for k in range(1, NS):
        total = total + drecv2[k].astype(F32)
    dsum2[0:DROWS, :] = total.reshape(DROWS, 128).astype(BF)
    dsum2[DROWS : NQ * DPIECE, :] = jnp.zeros((NQ * DPIECE - DROWS, 128), BF)
    d_dp = []
    for k in range(1, NQ):
        row = pl.multiple_of(lax.rem(q + k, NQ) * DPIECE, DPIECE)
        d_dp.append(
            send(
                dsum2.at[pl.ds(row, DPIECE), :], drecv3.at[k], dq_send.at[k], dq_recv.at[k],
                {"dp": dp_peer(k)},
            )
        )

    m2 = m_dp(2, m2)
    m0 = m_gather(0, m0)
    m1 = m_gather(1, m1)

    for copy in d_dp:
        copy.wait()
    q_row = pl.multiple_of(q * DPIECE, DPIECE)
    total = dsum2[pl.ds(q_row, DPIECE), :].astype(F32)
    for k in range(1, NQ):
        total = total + drecv3[k].astype(F32)
    dfull[pl.ds(q_row, DPIECE), :] = total.astype(BF)
    d_part = dfull.at[pl.ds(q_row, DPIECE), :]
    d_gather = [
        send(d_part, d_part, dg_send.at[k], dg_recv.at[k], {"dp": dp_peer(k)})
        for k in range(1, NQ)
    ]

    m2 = m_gather(2, m2)
    m0 = m_last(0, m0)
    m1 = m_last(1, m1)
    m_store(0, m0)
    m_store(1, m1)
    m2 = m_last(2, m2)
    for copy in d_gather:
        copy.wait()
    d_last = send(dfull, dother, pair_send.at[1], pair_recv.at[1], {"dp": other})
    m_store(2, m2)
    d_last.wait()
    mine = dfull[0:DROWS, :]
    theirs = dother[0:DROWS, :]
    dk_ref[:, 0:128] = jnp.where(core == 0, mine, theirs)
    dk_ref[:, 128:256] = jnp.where(core == 0, theirs, mine)


def finish(deep_ref, dk_ref, mk_ref, out_ref, dg_ref, mg_ref):
    deep_scale = math.sqrt(NQ * 2 * NS * 2 * 256)
    mid_scale = math.sqrt(NQ * 2 * NS * 4 * 1024)
    out_ref[...] = deep_ref[...]
    dg_ref[...] = dk_ref[...].astype(F32) * (1.0 / deep_scale)
    mg_ref[...] = mk_ref[0 : 27 * 64, :].astype(F32) * (1.0 / mid_scale)


def on_device(volume, first_kernel, mid_kernel, deep_kernel, deep_cotangent):
    vm = pl.BlockSpec(memory_space=pltpu.VMEM)
    hbm = pl.BlockSpec(memory_space=pltpu.HBM)
    dma = pltpu.SemaphoreType.DMA
    deep_out, deep_grad, mid_grad = pl.pallas_call(
        kernel,
        out_shape=(
            jax.ShapeDtypeStruct((2, 256, 256), BF),
            jax.ShapeDtypeStruct((DROWS, 256), BF),
            jax.ShapeDtypeStruct((MROWS, 128), BF),
        ),
        in_specs=[vm] + [hbm] * 4,
        out_specs=(vm, vm, vm),
        scratch_shapes=[
            pltpu.VMEM((4, 32, 128), BF),
            pltpu.VMEM((27 * 64, 128), BF),
            pltpu.VMEM((27 * 128, 256), BF),
            pltpu.VMEM((2, 256, 256), BF),
            pltpu.VMEM((2, 2, 32, 128), BF),
            pltpu.VMEM((48, 128), F32),
            pltpu.VMEM((144, 128), F32),
            pltpu.VMEM((3, 256, 128), BF),
            pltpu.VMEM((1152, 2048), BF),
            pltpu.VMEM((192, 2048), F32),
            pltpu.VMEM((2, 512, 128), F32),
            pltpu.VMEM((2304, 256), BF),
            pltpu.VMEM((6, 544, 256), BF),
            pltpu.VMEM((768, 3072), BF),
            pltpu.VMEM((4, 512, 256), F32),
            pltpu.VMEM((4, 512, 256), F32),
            pltpu.VMEM((2, 256, 128), BF),
            pltpu.VMEM((272, 256), F32),
            pltpu.VMEM((4, 288, 384), BF),
            pltpu.VMEM((1152, 1024), BF),
            pltpu.VMEM((2, 256, 128), BF),
            pltpu.VMEM((2, 256, 256), F32),
            pltpu.VMEM((2, 256, 256), BF),
            pltpu.VMEM((2, 256, 128), BF),
            pltpu.VMEM((2, 256, 128), BF),
            pltpu.VMEM((2, 288, 768), BF),
            pltpu.VMEM((2, 27, 128, 128), BF),
            pltpu.VMEM((27, 128, 128), BF),
            pltpu.VMEM((27, 128, 128), BF),
            pltpu.VMEM((NS, 27, CS, 128), BF),
            pltpu.VMEM((NQ * DPIECE, 128), BF),
            pltpu.VMEM((NQ, DPIECE, 128), BF),
            pltpu.VMEM((NQ * DPIECE, 128), BF),
            pltpu.VMEM((NQ * DPIECE, 128), BF),
            pltpu.VMEM((2048, 256), BF),
            pltpu.VMEM((MROWS, 128), BF),
            pltpu.VMEM((MHALF, 128), BF),
            pltpu.VMEM((MHALF, 128), BF),
            pltpu.VMEM((NS, MONE, 128), BF),
            pltpu.VMEM((NQ, MONE, 128), BF),
            pltpu.VMEM((MHALF, 128), BF),
            pltpu.VMEM((MHALF, 128), BF),
            dma((4,)), dma((6,)), dma((6,)), dma((2,)), dma((2,)),
            *[dma((8,)) for _ in range(6)],
            dma((3,)), dma((3,)),
            *[dma((3, 8)) for _ in range(6)],
            dma((3,)), dma((3,)),
        ],
        compiler_params=pltpu.CompilerParams(
            collective_id=0, has_side_effects=True, vmem_limit_bytes=44 * 1024 * 1024
        ),
    )(
        first_kernel.reshape(27, 4, 64),
        volume[0],
        mid_kernel.reshape(27 * 64, 128),
        deep_kernel.reshape(27 * 128, 256),
        deep_cotangent.reshape(2, 256, 256),
    )
    deep_out, deep_grad, mid_grad = pl.pallas_call(
        finish,
        out_shape=(
            jax.ShapeDtypeStruct((2, 256, 256), BF),
            jax.ShapeDtypeStruct((DROWS, 256), F32),
            jax.ShapeDtypeStruct((27 * 64, 128), F32),
        ),
        in_specs=[vm] * 3,
        out_specs=(vm, vm, vm),
        compiler_params=pltpu.CompilerParams(vmem_limit_bytes=8 * 1024 * 1024),
    )(deep_out, deep_grad, mid_grad)
    return (
        deep_out.reshape(1, 2, 16, 16, 256),
        deep_grad.reshape(3, 3, 3, CS, 256),
        mid_grad.reshape(3, 3, 3, 64, 128),
    )


def solution(mesh):
    in_specs = (P("dp", "space", None, None), P(), P(), P(), P("dp", "space", None, None, None))
    out_specs = (P("dp", "space", None, None, None), P(None, None, None, "space", None), P())
    return jax.shard_map(
        on_device, mesh=mesh, in_specs=in_specs, out_specs=out_specs, check_vma=False
    )
```

time: 82.9 us -> 65.9 us (0.79)
  Pallas kernels: 75.7 us -> 60 us
  other arithmetic: 4.51 us -> 0 us
  local copies, waits for them, and re-layouts: 1.79 us -> 4.93 us
    pallas_call x1, Pallas kernels: 75.7 us -> 58.7 us  [on_device(): pl.pallas_call(kernel, out_shape=(jax.ShapeDtypeStruct((2, 256, 256), BF)...]
    unnamed x3 -> x10, local copies, waits for them, and re-layouts: 0.71 us -> 4.93 us
    div x2 -> x0, other arithmetic: 3.76 us -> none  [the longest x1 2.03 us: on_device(): mid_grad[:27 * 64].astype(F32).reshape(3, 3, 3, 64, 128) / mid_scale]
    pallas_call x0 -> x1, Pallas kernels: none -> 1.22 us  [on_device(): pl.pallas_call(finish, out_shape=(jax.ShapeDtypeStruct((2, 256, 256), BF)...]
    another operation x4 -> x0, local copies, waits for them, and re-layouts: 0.96 us -> none  [the longest x2 0.92 us: on_device(): block = jnp.stack([even, odd], axis=3).reshape(9, 16, 128)]
where the time goes in v2:
time: 65.9 us; the launch traced here: 65.5 us
  Pallas kernels  60 us (91%)
  local copies, waits for them, and re-layouts  4.93 us (7%)
    pallas_call x1, Pallas kernels, on_device(): pl.pallas_call(kernel, out_shape=(jax.ShapeDtypeStruct((2, 256, 256), BF)...  58.7 us
    unnamed x10, local copies, waits for them, and re-layouts  4.93 us

profile of v2, /device:TPU:1, one launch (start us, length us, event | category | flops | bytes accessed | tf_op | source)
XLA Modules:
  0.0 65.5 jit_solution(2109726376478621703)
XLA Ops:
  0.6 0.0 copy-start
  0.6 1.5 %copy-done = bf16[3,3,3,128,256]{4,3,2,1,0:T(8,128)(2,1)S(1)} copy-done((bf16[3,3,3,128,256]{4,3,2,1,0:T(8,128)(2,1)S(1)}, bf16[3,3,3,128,256]{4,3,2,1,0:T(8,128)(2,1)}, u32[]{:S(2)}) %copy-start) | copy-done | bytes 1769496
  2.1 0.0 copy-start.1
  2.1 1.0 %copy-done.1 = bf16[3,3,3,64,128]{4,3,2,1,0:T(8,128)(2,1)S(1)} copy-done((bf16[3,3,3,64,128]{4,3,2,1,0:T(8,128)(2,1)S(1)}, bf16[3,3,3,64,128]{4,3,2,1,0:T(8,128)(2,1)}, u32[]{:S(2)}) %copy-start.1) | copy-done | bytes 442392
  3.1 0.0 copy-start.2
  3.1 0.9 %copy-done.2 = bf16[1,2,16,16,256]{4,3,2,1,0:T(8,128)(2,1)S(1)} copy-done((bf16[1,2,16,16,256]{4,3,2,1,0:T(8,128)(2,1)S(1)}, bf16[1,2,16,16,256]{4,3,2,1,0:T(8,128)(2,1)}, u32[]{:S(2)}) %copy-start.2) | copy-done | bytes 262168
  4.1 0.0 copy-start.3
  4.1 0.8 %copy-done.3 = bf16[1,4,32,128]{3,2,1,0:T(8,128)(2,1)S(1)} copy-done((bf16[1,4,32,128]{3,2,1,0:T(8,128)(2,1)S(1)}, bf16[1,4,32,128]{3,2,1,0:T(8,128)(2,1)}, u32[]{:S(2)}) %copy-start.3) | copy-done | bytes 32792
  4.8 0.0 copy-start.4
  4.8 0.7 %copy-done.4 = bf16[3,3,3,4,64]{4,3,2,1,0:T(4,128)(2,1)S(1)} copy-done((bf16[3,3,3,4,64]{4,3,2,1,0:T(4,128)(2,1)S(1)}, bf16[3,3,3,4,64]{4,3,2,1,0:T(4,128)(2,1)}, u32[]{:S(2)}) %copy-start.4) | copy-done | bytes 13848
  5.6 58.7 %shard_map.76 = (bf16[2,256,256]{2,1,0:T(8,128)(2,1)S(1)}, bf16[432,256]{1,0:T(8,128)(2,1)S(1)}, bf16[1792,128]{1,0:T(8,128)(2,1)S(1)}) custom-call(bf16[27,4,64]{2,1,0:T(4,128)(2,1)S(1)} %bitcast.12, bf16[4,32,128]{2,1,0:T(8,128)(2,1)S(1)} %bitcast.11, bf16[1728,128]{1,0:T(8,128)(2,1)S(1)} %bitcast.9, bf16[3456,256]{1,0:T(8,128)(2,1)S(1)} %bitcast.8, ...), custom_call_target="tpu_custom_call" | custom-call | tf_op jit(solution)/shard_map/pallas_call | solution.py:522
  64.3 1.2 %shard_map.77 = (bf16[2,256,256]{2,1,0:T(8,128)(2,1)}, f32[432,256]{1,0:T(8,128)}, f32[1728,128]{1,0:T(8,128)}) custom-call(bf16[2,256,256]{2,1,0:T(8,128)(2,1)S(1)} %get-tuple-element.9.deep_ref, bf16[432,256]{1,0:T(8,128)(2,1)S(1)} %get-tuple-element.10.dk_ref, bf16[1792,128]{1,0:T(8,128)(2,1)S(1)} %get-tuple-element.11.mk_ref), custom_call_target="tpu_custom_call" | custom-call | tf_op jit(solution)/shard_map/pallas_call | solution.py:590
Async XLA Ops:
  0.6 1.5 %copy-start = (bf16[3,3,3,128,256]{4,3,2,1,0:T(8,128)(2,1)S(1)}, bf16[3,3,3,128,256]{4,3,2,1,0:T(8,128)(2,1)}, u32[]{:S(2)}) copy-start(bf16[3,3,3,128,256]{4,3,2,1,0:T(8,128)(2,1)} %param.8) | copy-start | bytes 5308420
  2.1 1.0 %copy-start.1 = (bf16[3,3,3,64,128]{4,3,2,1,0:T(8,128)(2,1)S(1)}, bf16[3,3,3,64,128]{4,3,2,1,0:T(8,128)(2,1)}, u32[]{:S(2)}) copy-start(bf16[3,3,3,64,128]{4,3,2,1,0:T(8,128)(2,1)} %param.7) | copy-start | bytes 1327108
  3.1 0.9 %copy-start.2 = (bf16[1,2,16,16,256]{4,3,2,1,0:T(8,128)(2,1)S(1)}, bf16[1,2,16,16,256]{4,3,2,1,0:T(8,128)(2,1)}, u32[]{:S(2)}) copy-start(bf16[1,2,16,16,256]{4,3,2,1,0:T(8,128)(2,1)} %param.9) | copy-start | bytes 786436
  4.1 0.8 %copy-start.3 = (bf16[1,4,32,128]{3,2,1,0:T(8,128)(2,1)S(1)}, bf16[1,4,32,128]{3,2,1,0:T(8,128)(2,1)}, u32[]{:S(2)}) copy-start(bf16[1,4,32,128]{3,2,1,0:T(8,128)(2,1)} %param.5) | copy-start | bytes 98308
  4.8 0.7 %copy-start.4 = (bf16[3,3,3,4,64]{4,3,2,1,0:T(4,128)(2,1)S(1)}, bf16[3,3,3,4,64]{4,3,2,1,0:T(4,128)(2,1)}, u32[]{:S(2)}) copy-start(bf16[3,3,3,4,64]{4,3,2,1,0:T(4,128)(2,1)} %param.6) | copy-start | bytes 41476

commit v3 on v2

--- a/solution.py
+++ b/solution.py
@@ -18,6 +18,7 @@
 CS = 128 // NS
 DROWS = 27 * CS
 DPIECE = 64
+DQUARTER = 28 * 32
 MROWS = 28 * 64
 MHALF = MROWS // 2
 MPARTS = ((0, 512), (512, 512), (1024, 768))
@@ -65,14 +66,41 @@
     def dp_peer(k):
         return lax.rem(q + k, NQ) * 2 + core
 
+    first_core = core == 0
+    y_low = s % 2
+    z_chip = s // 2
+    x_chip = q % 4
+    y_high = q // 4
+    ring = jnp.where(first_core, z_chip, x_chip)
+
+    def ring_peer(k):
+        place = lax.rem(ring + k, 4)
+        return place, {
+            "dp": jnp.where(first_core, d, (y_high * 4 + place) * 2 + core),
+            "space": jnp.where(first_core, place * 2 + y_low, s),
+        }
+
+    def plane_peer(k):
+        a = jnp.where(first_core, lax.rem(y_low + k // 8, 2), lax.rem(s + k // 2, 8))
+        b = jnp.where(first_core, lax.rem(q + k % 8, 8), lax.rem(y_high + k % 2, 2))
+        return jnp.where(first_core, a * 8 + b, a * 2 + b), {
+            "dp": jnp.where(first_core, b, b * 4 + x_chip) * 2 + core,
+            "space": jnp.where(first_core, z_chip * 2 + a, a),
+        }
+
     up = space_peer(1)
     down = space_peer(NS - 1)
 
     barrier = pltpu.get_barrier_semaphore()
-    for k in (1, NS - 1, *range(2, NS - 1)):
-        pl.semaphore_signal(barrier, inc=1, device_id={"space": space_peer(k)}, device_id_type=MESH)
-    for k in range(1, NQ):
-        pl.semaphore_signal(barrier, inc=1, device_id={"dp": dp_peer(k)}, device_id_type=MESH)
+    for k in range(1, 16):
+        pl.semaphore_signal(barrier, inc=1, device_id=plane_peer(k)[1], device_id_type=MESH)
+    for k in range(6):
+        place = lax.rem(ring + 1 + k // 2, 4)
+        device = {
+            "dp": jnp.where(first_core, d, ((k % 2) * 4 + place) * 2 + core),
+            "space": jnp.where(first_core, place * 2 + k % 2, s),
+        }
+        pl.semaphore_signal(barrier, inc=1, device_id=device, device_id_type=MESH)
     pl.semaphore_signal(barrier, inc=1, device_id={"dp": other}, device_id_type=MESH)
 
     loads = []
@@ -114,7 +142,7 @@
                 tmat[base + 16 * (m + 1) : base + 16 * (m + 2), hi] = tiles[3]
 
     loads[0].wait()
-    pl.semaphore_wait(barrier, NS - 1 + NQ - 1 + 1)
+    pl.semaphore_wait(barrier, 15 + 6 + 1)
 
     v_down = send(vol_ref.at[0:2], vhalo.at[1], halo_send.at[0], halo_recv.at[0], {"space": down})
     v_up = send(vol_ref.at[2:4], vhalo.at[0], halo_send.at[1], halo_recv.at[1], {"space": up})
@@ -325,16 +353,25 @@
     back = [back_taps(0, 1) + back_taps(1, 0), back_taps(1, 1) + back_taps(0, 2)]
 
     d_pair.wait()
-    dsum1[...] = (dbuf[core].astype(F32) + drecv1[...].astype(F32)).astype(BF)
-    d_space = []
-    for k in range(1, NS):
-        row = pl.multiple_of(space_peer(k) * CS, CS)
-        d_space.append(
-            send(
-                dsum1.at[:, pl.ds(row, CS), :], drecv2.at[k], ds_send.at[k], ds_recv.at[k],
-                {"space": space_peer(k)},
-            )
-        )
+    dsum = (dbuf[core].astype(F32) + drecv1[...].astype(F32)).astype(BF)
+
+    @pl.when(first_core)
+    def _():
+        for place in range(4):
+            dsum1[place, 0:864, :] = dsum[:, 32 * place : 32 * place + 32, :].reshape(864, 128)
+            dsum1[place, 864:896, :] = jnp.zeros((32, 128), BF)
+
+    @pl.when(jnp.logical_not(first_core))
+    def _():
+        for place in range(4):
+            taps = 7 if place < 3 else 6
+            dsum1[place, 0 : taps * 128, :] = dsum[7 * place : 7 * place + taps].reshape(taps * 128, 128)
+        dsum1[3, 768:896, :] = jnp.zeros((128, 128), BF)
+
+    d_ring = []
+    for k in range(1, 4):
+        place, device = ring_peer(k)
+        d_ring.append(send(dsum1.at[place], drecv2.at[k], ds_send.at[k], ds_recv.at[k], device))
 
     out_ref[...] = act(predeep[...]).astype(BF)
 
@@ -455,38 +492,46 @@
     m0 = m_dp(0, m0)
     m1 = m_dp(1, m1)
 
-    for copy in d_space:
+    for copy in d_ring:
         copy.wait()
-    own_row = pl.multiple_of(s * CS, CS)
-    total = dsum1[:, pl.ds(own_row, CS), :].astype(F32)
-    for k in range(1, NS):
+    total = dsum1[ring].astype(F32)
+    for k in range(1, 4):
         total = total + drecv2[k].astype(F32)
-    dsum2[0:DROWS, :] = total.reshape(DROWS, 128).astype(BF)
-    dsum2[DROWS : NQ * DPIECE, :] = jnp.zeros((NQ * DPIECE - DROWS, 128), BF)
-    d_dp = []
-    for k in range(1, NQ):
-        row = pl.multiple_of(lax.rem(q + k, NQ) * DPIECE, DPIECE)
-        d_dp.append(
-            send(
-                dsum2.at[pl.ds(row, DPIECE), :], drecv3.at[k], dq_send.at[k], dq_recv.at[k],
-                {"dp": dp_peer(k)},
-            )
-        )
+    total = total.astype(BF)
+
+    @pl.when(first_core)
+    def _():
+        rows = total.reshape(28, 2, 16, 128)
+        for a in range(2):
+            for b in range(7):
+                dsum2[a * 8 + b] = rows[4 * b : 4 * b + 4, a].reshape(64, 128)
+            dsum2[a * 8 + 7] = jnp.zeros((64, 128), BF)
+
+    @pl.when(jnp.logical_not(first_core))
+    def _():
+        rows = total.reshape(7, 8, 16, 128)
+        for a in range(8):
+            dsum2[a * 2] = rows[0:4, a].reshape(64, 128)
+            dsum2[a * 2 + 1, 0:48, :] = rows[4:7, a].reshape(48, 128)
+            dsum2[a * 2 + 1, 48:64, :] = jnp.zeros((16, 128), BF)
+
+    d_plane = []
+    for k in range(1, 16):
+        place, device = plane_peer(k)
+        d_plane.append(send(dsum2.at[place], drecv3.at[k], dq_send.at[k], dq_recv.at[k], device))
 
     m2 = m_dp(2, m2)
     m0 = m_gather(0, m0)
     m1 = m_gather(1, m1)
 
-    for copy in d_dp:
+    for copy in d_plane:
         copy.wait()
-    q_row = pl.multiple_of(q * DPIECE, DPIECE)
-    total = dsum2[pl.ds(q_row, DPIECE), :].astype(F32)
-    for k in range(1, NQ):
+    total = dsum2[plane_peer(0)[0]].astype(F32)
+    for k in range(1, 16):
         total = total + drecv3[k].astype(F32)
-    dfull[pl.ds(q_row, DPIECE), :] = total.astype(BF)
-    d_part = dfull.at[pl.ds(q_row, DPIECE), :]
+    dfull[q] = total.astype(BF)
     d_gather = [
-        send(d_part, d_part, dg_send.at[k], dg_recv.at[k], {"dp": dp_peer(k)})
+        send(dfull.at[q], dfull.at[q], dg_send.at[k], dg_recv.at[k], {"dp": dp_peer(k)})
         for k in range(1, NQ)
     ]
 
@@ -501,10 +546,14 @@
     d_last = send(dfull, dother, pair_send.at[1], pair_recv.at[1], {"dp": other})
     m_store(2, m2)
     d_last.wait()
-    mine = dfull[0:DROWS, :]
-    theirs = dother[0:DROWS, :]
-    dk_ref[:, 0:128] = jnp.where(core == 0, mine, theirs)
-    dk_ref[:, 128:256] = jnp.where(core == 0, theirs, mine)
+    left = jnp.where(first_core, dfull[...], dother[...]).reshape(NQ * DPIECE, 128)
+    dk_ref[:, 0:128] = left[0:DROWS]
+    right = jnp.where(first_core, dother[...], dfull[...])
+    for place in range(4):
+        row = 7 * 16 * place
+        dk_ref[row : row + 64, 128:256] = right[place]
+        rest = 48 if place < 3 else 32
+        dk_ref[row + 64 : row + 64 + rest, 128:256] = right[4 + place, 0:rest]
 
 
 def finish(deep_ref, dk_ref, mk_ref, out_ref, dg_ref, mg_ref):
@@ -557,12 +606,12 @@
             pltpu.VMEM((2, 288, 768), BF),
             pltpu.VMEM((2, 27, 128, 128), BF),
             pltpu.VMEM((27, 128, 128), BF),
-            pltpu.VMEM((27, 128, 128), BF),
-            pltpu.VMEM((NS, 27, CS, 128), BF),
-            pltpu.VMEM((NQ * DPIECE, 128), BF),
+            pltpu.VMEM((4, DQUARTER, 128), BF),
+            pltpu.VMEM((4, DQUARTER, 128), BF),
+            pltpu.VMEM((16, DPIECE, 128), BF),
+            pltpu.VMEM((16, DPIECE, 128), BF),
             pltpu.VMEM((NQ, DPIECE, 128), BF),
-            pltpu.VMEM((NQ * DPIECE, 128), BF),
-            pltpu.VMEM((NQ * DPIECE, 128), BF),
+            pltpu.VMEM((NQ, DPIECE, 128), BF),
             pltpu.VMEM((2048, 256), BF),
             pltpu.VMEM((MROWS, 128), BF),
             pltpu.VMEM((MHALF, 128), BF),
@@ -572,7 +621,7 @@
             pltpu.VMEM((MHALF, 128), BF),
             pltpu.VMEM((MHALF, 128), BF),
             dma((4,)), dma((6,)), dma((6,)), dma((2,)), dma((2,)),
-            *[dma((8,)) for _ in range(6)],
+            dma((4,)), dma((4,)), dma((16,)), dma((16,)), dma((8,)), dma((8,)),
             dma((3,)), dma((3,)),
             *[dma((3, 8)) for _ in range(6)],
             dma((3,)), dma((3,)),
@@ -581,11 +630,11 @@
             collective_id=0, has_side_effects=True, vmem_limit_bytes=44 * 1024 * 1024
         ),
     )(
-        first_kernel.reshape(27, 4, 64),
+        *[pltpu.with_memory_space_constraint(x, pltpu.HBM) for x in (first_kernel.reshape(27, 4, 64),
         volume[0],
         mid_kernel.reshape(27 * 64, 128),
         deep_kernel.reshape(27 * 128, 256),
-        deep_cotangent.reshape(2, 256, 256),
+        deep_cotangent.reshape(2, 256, 256))],
     )
     deep_out, deep_grad, mid_grad = pl.pallas_call(
         finish,

time: 65.9 us -> 58.4 us (0.89)
  local copies, waits for them, and re-layouts: 4.93 us -> 0 us
  Pallas kernels: 60 us -> 57.5 us
    unnamed x10 -> x0, local copies, waits for them, and re-layouts: 4.93 us -> none
    pallas_call x1, Pallas kernels: 58.7 us -> 56.3 us  [on_device(): pl.pallas_call(kernel, out_shape=(jax.ShapeDtypeStruct((2, 256, 256), BF)...]
where the time goes in v3:
time: 58.4 us; the launch traced here: 58.2 us
  Pallas kernels  57.5 us (98%)
  between operations  0.64 us (1%)
    pallas_call x1, Pallas kernels, on_device(): pl.pallas_call(kernel, out_shape=(jax.ShapeDtypeStruct((2, 256, 256), BF)...  56.3 us
    pallas_call x1, Pallas kernels, on_device(): pl.pallas_call(finish, out_shape=(jax.ShapeDtypeStruct((2, 256, 256), BF)...  1.22 us

profile of v3, /device:TPU:1, one launch (start us, length us, event | category | flops | bytes accessed | tf_op | source)
XLA Modules:
  0.0 58.2 jit_solution(722467596666882253)
XLA Ops:
  0.6 56.3 %shard_map.76 = (bf16[2,256,256]{2,1,0:T(8,128)(2,1)S(1)}, bf16[432,256]{1,0:T(8,128)(2,1)S(1)}, bf16[1792,128]{1,0:T(8,128)(2,1)S(1)}) custom-call(bf16[27,4,64]{2,1,0:T(4,128)(2,1)} %bitcast.12, bf16[4,32,128]{2,1,0:T(8,128)(2,1)} %bitcast.11, bf16[1728,128]{1,0:T(8,128)(2,1)} %bitcast.9, bf16[3456,256]{1,0:T(8,128)(2,1)} %bitcast.8, ...), custom_call_target="tpu_custom_call" | custom-call | tf_op jit(solution)/shard_map/pallas_call | solution.py:571
  57.0 1.2 %shard_map.77 = (bf16[2,256,256]{2,1,0:T(8,128)(2,1)}, f32[432,256]{1,0:T(8,128)}, f32[1728,128]{1,0:T(8,128)}) custom-call(bf16[2,256,256]{2,1,0:T(8,128)(2,1)S(1)} %get-tuple-element.9.deep_ref, bf16[432,256]{1,0:T(8,128)(2,1)S(1)} %get-tuple-element.10.dk_ref, bf16[1792,128]{1,0:T(8,128)(2,1)S(1)} %get-tuple-element.11.mk_ref), custom_call_target="tpu_custom_call" | custom-call | tf_op jit(solution)/shard_map/pallas_call | solution.py:639

commit v4 on v3

--- a/solution.py
+++ b/solution.py
@@ -46,8 +46,8 @@
     fk_ref, vol_hbm, km_hbm, kd_hbm, cot_hbm,
     out_ref, dk_ref, mk_ref,
     vol_ref, km_ref, kd_ref, cot_ref,
-    vhalo, ef, vf, volb, tmat, ybuf, yst, wmid, xpad, xt, pre_mid, slope_mid,
-    phalo, pf, pcat, pt, pooled_send, predeep, grad, bsend, bhalo, gcat, dbuf, drecv1, dsum1,
+    vhalo, ef, vf, volb, tmat, ybuf, yst, wmid, xpad, pre_mid, slope_mid,
+    phalo, pf, pcat, pooled_send, predeep, grad, bsend, bhalo, gcat, dbuf, drecv1, dsum1,
     drecv2, dsum2, drecv3, dfull, dother, gmid, mbuf, mrecv1, msum1, mrecv2,
     mrecv3, mfull, mout,
     load_sem, halo_send, halo_recv, pair_send, pair_recv, ds_send, ds_recv, dq_send, dq_recv,
@@ -281,22 +281,12 @@
     predeep[0] = deep_taps(0, 1) + deep_taps(0, 2)
     predeep[1] = deep_taps(1, 0) + deep_taps(1, 1)
 
-    for b in range(3):
-        for i in range(6):
-            xt[b * 256 : (b + 1) * 256, i * 512 : (i + 1) * 512] = xpad[i, 16 * b : 16 * b + 512, :].T
-
     def slopes(i, c):
         slope_mid[i] = 0.125 * act_slope(pre_mid[i])
         return c
 
     lax.fori_loop(0, 4, slopes, 0)
 
-    def put_turned(i):
-        for b in range(3):
-            pt[b * 384 : (b + 1) * 384, i * 256 : (i + 1) * 256] = pcat[i, 16 * b : 16 * b + 256, :].T
-
-    put_turned(1)
-    put_turned(2)
     loads[3].wait()
 
     grow = lax.broadcasted_iota(jnp.int32, (256, 256), 0) % 16
@@ -341,11 +331,11 @@
             )
         )
 
-    put_turned(0)
-    put_turned(3)
     gown = grad[...].reshape(512, 256)
     for a in range(3):
-        term = dot(pt[:, a * 256 : a * 256 + 512], gown).astype(BF).reshape(9, 128, 256)
+        term = jnp.concatenate([
+            dot(pcat[a, 16 * b : 16 * b + 256, :], gown[:256], ((0,), (0,))) + dot(pcat[a + 1, 16 * b : 16 * b + 256, :], gown[256:], ((0,), (0,)))
+            for b in range(3)], axis=0).astype(BF).reshape(9, 128, 256)
         dbuf[0, 9 * a : 9 * a + 9] = term[:, :, :128]
         dbuf[1, 9 * a : 9 * a + 9] = term[:, :, 128:]
     d_pair = send(dbuf.at[1 - core], drecv1, pair_send.at[0], pair_recv.at[0], {"dp": other})
@@ -372,8 +362,6 @@
     for k in range(1, 4):
         place, device = ring_peer(k)
         d_ring.append(send(dsum1.at[place], drecv2.at[k], ds_send.at[k], ds_recv.at[k], device))
-
-    out_ref[...] = act(predeep[...]).astype(BF)
 
     for plane in (1, 0):
         b_copies[plane].wait()
@@ -387,9 +375,11 @@
             gmid[row : row + 512, :] = value.reshape(512, 256).astype(BF)
 
     def mid_grad(a):
-        part = dot(xt[:, a * 512 : a * 512 + 2048], gmid[...])
         for b in range(3):
-            r = part[b * 256 : (b + 1) * 256]
+            cells = jnp.concatenate(
+                [xpad[i + a, 16 * b : 16 * b + 512, :] for i in range(4)], axis=0
+            )
+            r = dot(cells, gmid[...], ((0,), (0,)))
             row = (a * 3 + b) * 192
             mbuf[row : row + 64, :] = (r[0:64, 128:] + r[192:256, :128]).astype(BF)
             mbuf[row + 64 : row + 128, :] = (r[0:64, :128] + r[64:128, 128:]).astype(BF)
@@ -488,6 +478,8 @@
     m2 = m_pair(2)
     m1 = m_space(1, m1)
     m2 = m_space(2, m2)
+
+    out_ref[...] = act(predeep[...]).astype(BF)
 
     m0 = m_dp(0, m0)
     m1 = m_dp(1, m1)
@@ -591,13 +583,11 @@
             pltpu.VMEM((2, 512, 128), F32),
             pltpu.VMEM((2304, 256), BF),
             pltpu.VMEM((6, 544, 256), BF),
-            pltpu.VMEM((768, 3072), BF),
             pltpu.VMEM((4, 512, 256), F32),
             pltpu.VMEM((4, 512, 256), F32),
             pltpu.VMEM((2, 256, 128), BF),
             pltpu.VMEM((272, 256), F32),
             pltpu.VMEM((4, 288, 384), BF),
-            pltpu.VMEM((1152, 1024), BF),
             pltpu.VMEM((2, 256, 128), BF),
             pltpu.VMEM((2, 256, 256), F32),
             pltpu.VMEM((2, 256, 256), BF),

time: 58.4 us -> 56.2 us (0.962)
  Pallas kernels: 57.5 us -> 55.3 us
    pallas_call x1, Pallas kernels: 56.3 us -> 54.1 us  [on_device(): pl.pallas_call(kernel, out_shape=(jax.ShapeDtypeStruct((2, 256, 256), BF)...]
where the time goes in v4:
time: 56.2 us; the launch traced here: 56 us
  Pallas kernels  55.3 us (98%)
  between operations  0.64 us (1%)
    pallas_call x1, Pallas kernels, on_device(): pl.pallas_call(kernel, out_shape=(jax.ShapeDtypeStruct((2, 256, 256), BF)...  54.1 us
    pallas_call x1, Pallas kernels, on_device(): pl.pallas_call(finish, out_shape=(jax.ShapeDtypeStruct((2, 256, 256), BF)...  1.22 us

profile of v4, /device:TPU:1, one launch (start us, length us, event | category | flops | bytes accessed | tf_op | source)
XLA Modules:
  0.0 56.0 jit_solution(11860544792591417604)
XLA Ops:
  0.6 54.1 %shard_map.76 = (bf16[2,256,256]{2,1,0:T(8,128)(2,1)S(1)}, bf16[432,256]{1,0:T(8,128)(2,1)S(1)}, bf16[1792,128]{1,0:T(8,128)(2,1)S(1)}) custom-call(bf16[27,4,64]{2,1,0:T(4,128)(2,1)} %bitcast.12, bf16[4,32,128]{2,1,0:T(8,128)(2,1)} %bitcast.11, bf16[1728,128]{1,0:T(8,128)(2,1)} %bitcast.9, bf16[3456,256]{1,0:T(8,128)(2,1)} %bitcast.8, ...), custom_call_target="tpu_custom_call" | custom-call | tf_op jit(solution)/shard_map/pallas_call | solution.py:563
  54.7 1.2 %shard_map.77 = (bf16[2,256,256]{2,1,0:T(8,128)(2,1)}, f32[432,256]{1,0:T(8,128)}, f32[1728,128]{1,0:T(8,128)}) custom-call(bf16[2,256,256]{2,1,0:T(8,128)(2,1)S(1)} %get-tuple-element.9.deep_ref, bf16[432,256]{1,0:T(8,128)(2,1)S(1)} %get-tuple-element.10.dk_ref, bf16[1792,128]{1,0:T(8,128)(2,1)S(1)} %get-tuple-element.11.mk_ref), custom_call_target="tpu_custom_call" | custom-call | tf_op jit(solution)/shard_map/pallas_call | solution.py:629

commit v5 on v4

--- a/solution.py
+++ b/solution.py
@@ -50,7 +50,7 @@
     phalo, pf, pcat, pooled_send, predeep, grad, bsend, bhalo, gcat, dbuf, drecv1, dsum1,
     drecv2, dsum2, drecv3, dfull, dother, gmid, mbuf, mrecv1, msum1, mrecv2,
     mrecv3, mfull, mout,
-    load_sem, halo_send, halo_recv, pair_send, pair_recv, ds_send, ds_recv, dq_send, dq_recv,
+    known, load_sem, halo_send, halo_recv, pair_send, pair_recv, ds_send, ds_recv, dq_send, dq_recv,
     dg_send, dg_recv, mp_send, mp_recv, ms_send, ms_recv, mq_send, mq_recv, mg_send, mg_recv,
     mo_send, mo_recv,
 ):
@@ -92,16 +92,16 @@
     down = space_peer(NS - 1)
 
     barrier = pltpu.get_barrier_semaphore()
-    for k in range(1, 16):
-        pl.semaphore_signal(barrier, inc=1, device_id=plane_peer(k)[1], device_id_type=MESH)
-    for k in range(6):
-        place = lax.rem(ring + 1 + k // 2, 4)
-        device = {
-            "dp": jnp.where(first_core, d, ((k % 2) * 4 + place) * 2 + core),
-            "space": jnp.where(first_core, place * 2 + k % 2, s),
-        }
-        pl.semaphore_signal(barrier, inc=1, device_id=device, device_id_type=MESH)
-    pl.semaphore_signal(barrier, inc=1, device_id={"dp": other}, device_id_type=MESH)
+    near = [{"space": up}, {"space": down}]
+    near += [{"space": lax.rem(s + k, NS)} for k in (2, NS - 2)]
+    near += [{"dp": (y_high * 4 + lax.rem(x_chip + k, 4)) * 2 + core} for k in (1, 3)]
+    near += [{"dp": lax.rem(q + 4, NQ) * 2 + core}, {"dp": other}]
+
+    def tell(sem):
+        for device in near:
+            pl.semaphore_signal(sem, inc=1, device_id=device, device_id_type=MESH)
+
+    tell(barrier)
 
     loads = []
     for i, (src, dst) in enumerate(
@@ -142,10 +142,12 @@
                 tmat[base + 16 * (m + 1) : base + 16 * (m + 2), hi] = tiles[3]
 
     loads[0].wait()
-    pl.semaphore_wait(barrier, 15 + 6 + 1)
+    pl.semaphore_wait(barrier, len(near))
 
     v_down = send(vol_ref.at[0:2], vhalo.at[1], halo_send.at[0], halo_recv.at[0], {"space": down})
     v_up = send(vol_ref.at[2:4], vhalo.at[0], halo_send.at[1], halo_recv.at[1], {"space": up})
+
+    tell(known.at[0])
 
     loads[1].wait()
     for ab in range(9):
@@ -220,6 +222,8 @@
     put_hidden(2)
     put_hidden(3)
 
+    pl.semaphore_wait(known.at[0], len(near))
+    tell(known.at[1])
     v_up.wait()
     put_volume(0, jnp.where(s == 0, 0.0, vhalo[0].astype(F32)).reshape(64, 128))
     first(0)
@@ -270,6 +274,8 @@
     put_hidden(5)
     pool(1)
 
+    pl.semaphore_wait(known.at[1], len(near))
+    tell(known.at[2])
     loads[2].wait()
 
     def deep_taps(plane, a):
@@ -338,6 +344,7 @@
             for b in range(3)], axis=0).astype(BF).reshape(9, 128, 256)
         dbuf[0, 9 * a : 9 * a + 9] = term[:, :, :128]
         dbuf[1, 9 * a : 9 * a + 9] = term[:, :, 128:]
+    pl.semaphore_wait(known.at[2], len(near))
     d_pair = send(dbuf.at[1 - core], drecv1, pair_send.at[0], pair_recv.at[0], {"dp": other})
 
     back = [back_taps(0, 1) + back_taps(1, 0), back_taps(1, 1) + back_taps(0, 2)]
@@ -610,6 +617,7 @@
             pltpu.VMEM((NQ, MONE, 128), BF),
             pltpu.VMEM((MHALF, 128), BF),
             pltpu.VMEM((MHALF, 128), BF),
+            pltpu.SemaphoreType.REGULAR((3,)),
             dma((4,)), dma((6,)), dma((6,)), dma((2,)), dma((2,)),
             dma((4,)), dma((4,)), dma((16,)), dma((16,)), dma((8,)), dma((8,)),
             dma((3,)), dma((3,)),

time: 56.2 us -> 55.6 us (0.989)
  Pallas kernels: 55.3 us -> 54.7 us
    pallas_call x1, Pallas kernels: 54.1 us -> 53.5 us  [on_device(): pl.pallas_call(kernel, out_shape=(jax.ShapeDtypeStruct((2, 256, 256), BF)...]
where the time goes in v5:
time: 55.6 us; the launch traced here: 55.4 us
  Pallas kernels  54.7 us (98%)
  between operations  0.64 us (1%)
    pallas_call x1, Pallas kernels, on_device(): pl.pallas_call(kernel, out_shape=(jax.ShapeDtypeStruct((2, 256, 256), BF)...  53.5 us
    pallas_call x1, Pallas kernels, on_device(): pl.pallas_call(finish, out_shape=(jax.ShapeDtypeStruct((2, 256, 256), BF)...  1.22 us

profile of v5, /device:TPU:1, one launch (start us, length us, event | category | flops | bytes accessed | tf_op | source)
XLA Modules:
  0.0 55.4 jit_solution(11658252376504230738)
XLA Ops:
  0.6 53.5 %shard_map.76 = (bf16[2,256,256]{2,1,0:T(8,128)(2,1)S(1)}, bf16[432,256]{1,0:T(8,128)(2,1)S(1)}, bf16[1792,128]{1,0:T(8,128)(2,1)S(1)}) custom-call(bf16[27,4,64]{2,1,0:T(4,128)(2,1)} %bitcast.12, bf16[4,32,128]{2,1,0:T(8,128)(2,1)} %bitcast.11, bf16[1728,128]{1,0:T(8,128)(2,1)} %bitcast.9, bf16[3456,256]{1,0:T(8,128)(2,1)} %bitcast.8, ...), custom_call_target="tpu_custom_call" | custom-call | tf_op jit(solution)/shard_map/pallas_call | solution.py:570
  54.1 1.2 %shard_map.77 = (bf16[2,256,256]{2,1,0:T(8,128)(2,1)}, f32[432,256]{1,0:T(8,128)}, f32[1728,128]{1,0:T(8,128)}) custom-call(bf16[2,256,256]{2,1,0:T(8,128)(2,1)S(1)} %get-tuple-element.9.deep_ref, bf16[432,256]{1,0:T(8,128)(2,1)S(1)} %get-tuple-element.10.dk_ref, bf16[1792,128]{1,0:T(8,128)(2,1)S(1)} %get-tuple-element.11.mk_ref), custom_call_target="tpu_custom_call" | custom-call | tf_op jit(solution)/shard_map/pallas_call | solution.py:637

commit v6 on v5

--- a/solution.py
+++ b/solution.py
@@ -226,8 +226,29 @@
     tell(known.at[1])
     v_up.wait()
     put_volume(0, jnp.where(s == 0, 0.0, vhalo[0].astype(F32)).reshape(64, 128))
-    first(0)
+    v_down.wait()
+    put_volume(192, jnp.where(s == NS - 1, 0.0, vhalo[1].astype(F32)).reshape(64, 128))
+
+    def outer(m, c):
+        lhs = jnp.concatenate(
+            [
+                jnp.concatenate(
+                    [volb[b, 32 * (p + a) : 32 * (p + a) + 64, :] for p in (0, 4)], axis=0
+                )
+                for a in range(3)
+                for b in range(3)
+            ],
+            axis=1,
+        )
+        col = pl.multiple_of(m * 256, 256)
+        value = act(dot(lhs, tmat[:, pl.ds(col, 256)]))
+        ybuf[0:64, pl.ds(col, 256)] = value[0:64]
+        ybuf[128:192, pl.ds(col, 256)] = value[64:128]
+        return c
+
+    lax.fori_loop(0, 8, outer, 0)
     ybuf[0:32, :] = jnp.where(s == 0, 0.0, ybuf[0:32, :])
+    ybuf[160:192, :] = jnp.where(s == NS - 1, 0.0, ybuf[160:192, :])
     put_hidden(0)
     put_hidden(1)
 
@@ -266,10 +287,6 @@
 
     pool(0)
 
-    v_down.wait()
-    put_volume(192, jnp.where(s == NS - 1, 0.0, vhalo[1].astype(F32)).reshape(64, 128))
-    first(4)
-    ybuf[160:192, :] = jnp.where(s == NS - 1, 0.0, ybuf[160:192, :])
     put_hidden(4)
     put_hidden(5)
     pool(1)
@@ -539,11 +556,10 @@
     m1 = m_last(1, m1)
     m_store(0, m0)
     m_store(1, m1)
-    m2 = m_last(2, m2)
     for copy in d_gather:
         copy.wait()
     d_last = send(dfull, dother, pair_send.at[1], pair_recv.at[1], {"dp": other})
-    m_store(2, m2)
+    m2 = m_last(2, m2)
     d_last.wait()
     left = jnp.where(first_core, dfull[...], dother[...]).reshape(NQ * DPIECE, 128)
     dk_ref[:, 0:128] = left[0:DROWS]
@@ -553,6 +569,7 @@
         dk_ref[row : row + 64, 128:256] = right[place]
         rest = 48 if place < 3 else 32
         dk_ref[row + 64 : row + 64 + rest, 128:256] = right[4 + place, 0:rest]
+    m_store(2, m2)
 
 
 def finish(deep_ref, dk_ref, mk_ref, out_ref, dg_ref, mg_ref):

time: 55.6 us -> 55.2 us (level)
  no operation moved by 1% of the time
where the time goes in v6:
time: 55.2 us; the launch traced here: 55 us
  Pallas kernels  54.3 us (98%)
  between operations  0.64 us (1%)
    pallas_call x1, Pallas kernels, on_device(): pl.pallas_call(kernel, out_shape=(jax.ShapeDtypeStruct((2, 256, 256), BF)...  53.1 us
    pallas_call x1, Pallas kernels, on_device(): pl.pallas_call(finish, out_shape=(jax.ShapeDtypeStruct((2, 256, 256), BF)...  1.22 us

profile of v6, /device:TPU:1, one launch (start us, length us, event | category | flops | bytes accessed | tf_op | source)
XLA Modules:
  0.0 55.0 jit_solution(9369444178323276013)
XLA Ops:
  0.6 53.1 %shard_map.76 = (bf16[2,256,256]{2,1,0:T(8,128)(2,1)S(1)}, bf16[432,256]{1,0:T(8,128)(2,1)S(1)}, bf16[1792,128]{1,0:T(8,128)(2,1)S(1)}) custom-call(bf16[27,4,64]{2,1,0:T(4,128)(2,1)} %bitcast.12, bf16[4,32,128]{2,1,0:T(8,128)(2,1)} %bitcast.11, bf16[1728,128]{1,0:T(8,128)(2,1)} %bitcast.9, bf16[3456,256]{1,0:T(8,128)(2,1)} %bitcast.8, ...), custom_call_target="tpu_custom_call" | custom-call | tf_op jit(solution)/shard_map/pallas_call | solution.py:587
  53.7 1.2 %shard_map.77 = (bf16[2,256,256]{2,1,0:T(8,128)(2,1)}, f32[432,256]{1,0:T(8,128)}, f32[1728,128]{1,0:T(8,128)}) custom-call(bf16[2,256,256]{2,1,0:T(8,128)(2,1)S(1)} %get-tuple-element.9.deep_ref, bf16[432,256]{1,0:T(8,128)(2,1)S(1)} %get-tuple-element.10.dk_ref, bf16[1792,128]{1,0:T(8,128)(2,1)S(1)} %get-tuple-element.11.mk_ref), custom_call_target="tpu_custom_call" | custom-call | tf_op jit(solution)/shard_map/pallas_call | solution.py:654

commit v7 on v6

--- a/solution.py
+++ b/solution.py
@@ -354,19 +354,24 @@
             )
         )
 
+    pl.semaphore_wait(known.at[2], len(near))
     gown = grad[...].reshape(512, 256)
+    d_pair = []
     for a in range(3):
         term = jnp.concatenate([
             dot(pcat[a, 16 * b : 16 * b + 256, :], gown[:256], ((0,), (0,))) + dot(pcat[a + 1, 16 * b : 16 * b + 256, :], gown[256:], ((0,), (0,)))
             for b in range(3)], axis=0).astype(BF).reshape(9, 128, 256)
         dbuf[0, 9 * a : 9 * a + 9] = term[:, :, :128]
         dbuf[1, 9 * a : 9 * a + 9] = term[:, :, 128:]
-    pl.semaphore_wait(known.at[2], len(near))
-    d_pair = send(dbuf.at[1 - core], drecv1, pair_send.at[0], pair_recv.at[0], {"dp": other})
-
-    back = [back_taps(0, 1) + back_taps(1, 0), back_taps(1, 1) + back_taps(0, 2)]
-
-    d_pair.wait()
+        d_pair.append(
+            send(
+                dbuf.at[1 - core, 9 * a : 9 * a + 9], drecv1.at[9 * a : 9 * a + 9],
+                pair_send.at[2 + a], pair_recv.at[2 + a], {"dp": other},
+            )
+        )
+
+    for copy in d_pair:
+        copy.wait()
     dsum = (dbuf[core].astype(F32) + drecv1[...].astype(F32)).astype(BF)
 
     @pl.when(first_core)
@@ -386,6 +391,8 @@
     for k in range(1, 4):
         place, device = ring_peer(k)
         d_ring.append(send(dsum1.at[place], drecv2.at[k], ds_send.at[k], ds_recv.at[k], device))
+
+    back = [back_taps(0, 1) + back_taps(1, 0), back_taps(1, 1) + back_taps(0, 2)]
 
     for plane in (1, 0):
         b_copies[plane].wait()
@@ -635,7 +642,7 @@
             pltpu.VMEM((MHALF, 128), BF),
             pltpu.VMEM((MHALF, 128), BF),
             pltpu.SemaphoreType.REGULAR((3,)),
-            dma((4,)), dma((6,)), dma((6,)), dma((2,)), dma((2,)),
+            dma((4,)), dma((6,)), dma((6,)), dma((5,)), dma((5,)),
             dma((4,)), dma((4,)), dma((16,)), dma((16,)), dma((8,)), dma((8,)),
             dma((3,)), dma((3,)),
             *[dma((3, 8)) for _ in range(6)],

time: 55.2 us -> 54.5 us (0.987)
  Pallas kernels: 54.3 us -> 53.7 us
    pallas_call x1, Pallas kernels: 53.1 us -> 52.5 us  [on_device(): pl.pallas_call(kernel, out_shape=(jax.ShapeDtypeStruct((2, 256, 256), BF)...]
where the time goes in v7:
time: 54.5 us; the launch traced here: 54.3 us
  Pallas kernels  53.7 us (99%)
  between operations  0.64 us (1%)
    pallas_call x1, Pallas kernels, on_device(): pl.pallas_call(kernel, out_shape=(jax.ShapeDtypeStruct((2, 256, 256), BF)...  52.5 us
    pallas_call x1, Pallas kernels, on_device(): pl.pallas_call(finish, out_shape=(jax.ShapeDtypeStruct((2, 256, 256), BF)...  1.22 us

profile of v7, /device:TPU:1, one launch (start us, length us, event | category | flops | bytes accessed | tf_op | source)
XLA Modules:
  0.0 54.3 jit_solution(3063423190288933218)
XLA Ops:
  0.6 52.5 %shard_map.76 = (bf16[2,256,256]{2,1,0:T(8,128)(2,1)S(1)}, bf16[432,256]{1,0:T(8,128)(2,1)S(1)}, bf16[1792,128]{1,0:T(8,128)(2,1)S(1)}) custom-call(bf16[27,4,64]{2,1,0:T(4,128)(2,1)} %bitcast.12, bf16[4,32,128]{2,1,0:T(8,128)(2,1)} %bitcast.11, bf16[1728,128]{1,0:T(8,128)(2,1)} %bitcast.9, bf16[3456,256]{1,0:T(8,128)(2,1)} %bitcast.8, ...), custom_call_target="tpu_custom_call" | custom-call | tf_op jit(solution)/shard_map/pallas_call | solution.py:594
  53.1 1.2 %shard_map.77 = (bf16[2,256,256]{2,1,0:T(8,128)(2,1)}, f32[432,256]{1,0:T(8,128)}, f32[1728,128]{1,0:T(8,128)}) custom-call(bf16[2,256,256]{2,1,0:T(8,128)(2,1)S(1)} %get-tuple-element.9.deep_ref, bf16[432,256]{1,0:T(8,128)(2,1)S(1)} %get-tuple-element.10.dk_ref, bf16[1792,128]{1,0:T(8,128)(2,1)S(1)} %get-tuple-element.11.mk_ref), custom_call_target="tpu_custom_call" | custom-call | tf_op jit(solution)/shard_map/pallas_call | solution.py:661
